TPU v7x, 32 devices: a whole 2x2x4 slice. The times are simulated.
32 devices in a mesh: cross: 16 (over z, y, core), height: 2 (over x).
Axes of the slice: x: 2, y: 2, z: 4, core: 2. Of those that a mesh axis runs over, the one named last changes fastest.
Arguments:
- state: float32 [4, 16, 256, 512], P(None, 'height', 'cross'), may hold values from -6 to 6
- turbulence: bfloat16 [2, 16, 256, 512], P(None, 'height', 'cross'), may hold values from -2 to 2
- wind: float32 [16], P('height'), may hold values from 0.05 to 0.35
- ground_admittance: float32 [256, 512], P('cross'), may hold values from 0.2 to 2
- ground_kind: int32 [256, 512], P('cross'), may hold values 0 or 1
- drift_cells: int32 [2, 16], P(None, 'height'), may hold values from 0 to 255
- drift_eighths: int32 [2, 16], P(None, 'height'), may hold values from 0 to 7
Outputs:
- state_out: float32 [4, 16, 256, 512], P(None, 'height', 'cross')
All inputs are finite; a program needn't handle non-finite values. No bound on the sum of `ground_kind` on one device may be relied on, other than what follows from the above.
Results may differ from a plain program's by a relative error of at most 0.0015.
Values may be sent and summed in bfloat16 or wider, within the bound.
A program may use at most 64 MiB of HBM per device.

v0:
```python
import jax
import jax.numpy as jnp
from jax import lax
from jax.sharding import PartitionSpec as P

section_keep = (0.0, -5.0 / 9.0, -153.0 / 128.0)
section_gain = (1.0 / 3.0, 15.0 / 16.0, 8.0 / 15.0)
time_step = 0.4


def from_behind(value, axis, by):
    peers = lax.axis_size(axis)
    return lax.ppermute(value, axis, [(i, (i + by) % peers) for i in range(peers)])


def for_sending(value):

    def short(part):
        return part.astype(jnp.bfloat16) if part.dtype == jnp.float32 else part

    return jax.tree.map(short, value)


def padded_2(cells, sides, width):
    for axis, dim in sides:
        count = lax.axis_size(axis)
        ends = count - 1
        head = lax.slice_in_dim(cells, 0, width, axis=dim)
        tail = lax.slice_in_dim(cells, cells.shape[dim] - width, cells.shape[dim], axis=dim)
        cells = jnp.concatenate(
            [
                lax.ppermute(tail, axis, [(i, (i + 1) % count) for i in range(ends)]),
                cells,
                lax.ppermute(head, axis, [((i + 1) % count, i) for i in range(ends)]),
            ],
            axis=dim,
        )
    return cells


def bit_set(cells, span):
    return cells // span % 2 == 1


def roll_rows(block, count):
    moved = from_behind(block[..., -count:, :], "cross", 1)
    return jnp.concatenate([moved, block[..., :-count, :]], axis=-2)


def roll_edge(block):
    moved = from_behind(block[..., -1:, :], "cross", 1)
    return jnp.concatenate([moved, block[..., :-1, :]], axis=-2)


def place(turbulence, cells, eighths):
    rows = turbulence.shape[-2]
    devices = lax.axis_size("cross")
    moved = turbulence
    for level in range(rows.bit_length() - 1):
        span = 2**level
        moved = jnp.where(bit_set(cells, span), roll_rows(moved, span), moved)
    for level in range(devices.bit_length() - 1):
        hops = 2**level
        shifted = from_behind(moved, "cross", hops)
        moved = jnp.where(bit_set(cells, hops * rows), shifted, moved)
    first = moved.astype(jnp.float32)
    second = roll_edge(moved).astype(jnp.float32)
    weight = eighths.astype(jnp.float32) / 8.0
    return (1.0 - weight) * first + weight * second


def along_range(field):
    padded = jnp.pad(field, [(0, 0)] * (field.ndim - 1) + [(1, 1)])
    return 0.5 * (padded[..., 2:] - padded[..., :-2])


def rates(state, advect, squared, ground):
    pressure, vel_up = (state[0], state[3])
    sideways = padded_2(for_sending(jnp.stack([pressure, state[2]])), (("cross", 2),), 1)
    vertical = padded_2(for_sending(jnp.stack([pressure, vel_up])), (("height", 1),), 1)
    cross_p = sideways[0]
    cross_v = sideways[1]
    upper_p = vertical[0]
    upper_w = vertical[1]
    bottom = lax.axis_index("height") == 0
    low_p = jnp.where(bottom, pressure[0], upper_p[0])
    low_w = jnp.where(bottom, ground * pressure[0] - vel_up[0], upper_w[0])
    upper_p = jnp.concatenate([low_p[None], upper_p[1:]], axis=0)
    upper_w = jnp.concatenate([low_w[None], upper_w[1:]], axis=0)
    dy_p = 0.5 * (cross_p[:, 2:] - cross_p[:, :-2])
    dy_v = 0.5 * (cross_v[:, 2:] - cross_v[:, :-2])
    dz_p = 0.5 * (upper_p[2:] - upper_p[:-2])
    dz_w = 0.5 * (upper_w[2:] - upper_w[:-2])
    slope = along_range(state)
    rate_p = -advect * slope[0] - squared * (slope[1] + dy_v + dz_w)
    rate_u = -advect * slope[1] - slope[0]
    rate_v = -advect * slope[2] - dy_p
    rate_w = -advect * slope[3] - dz_p
    return jnp.stack([rate_p, rate_u, rate_v, rate_w])


def body(state, turbulence, wind, ground_admittance, ground_kind, drift_cells, drift_eighths):
    ground = 2.0 * ground_admittance * ground_kind.astype(jnp.float32)
    levels = turbulence.shape[1]
    steps = drift_cells.shape[0]
    current = state
    for step in range(steps):
        frozen = place(
            turbulence,
            drift_cells[step].reshape(1, levels, 1, 1),
            drift_eighths[step].reshape(1, levels, 1, 1),
        )
        advect = wind[:, None, None] + frozen[0]
        squared = (1.0 + frozen[1]) * (1.0 + frozen[1])
        change = jnp.zeros_like(current)
        for section in range(3):
            change = section_keep[section] * change + time_step * rates(
                current, advect, squared, ground
            )
            current = current + section_gain[section] * change
    return current


def solution(mesh):
    placed = (
        P(None, "height", "cross", None),
        P(None, "height", "cross", None),
        P("height"),
        P("cross", None),
        P("cross", None),
        P(None, "height"),
        P(None, "height"),
    )
    return jax.shard_map(
        body,
        mesh=mesh,
        in_specs=placed,
        out_specs=P(None, "height", "cross", None),
        check_vma=False,
    )
```

profile of v0, /device:TPU:8, one launch (start us, length us, event | category | flops | bytes accessed | tf_op | source)
XLA Modules:
  0.0 173.1 jit_solution(9216849451471594158)
XLA Ops:
  0.0 2.9 %fusion.1 = (f32[4,8,16,512]{3,2,1,0:T(8,128)S(1)}, bf16[4,8,16,512]{3,2,1,0:T(8,128)(2,1)S(1)}) fusion(f32[4,8,16,512]{3,2,1,0:T(8,128)} %param.7), kind=kLoop, calls=%fused_computation.13 | loop fusion | flops 786432 | bytes 2621440 | tf_op jit(solution)/shard_map/mul | solution.py:74
  3.0 1.3 collective-permute-start.11
  4.3 4.5 %collective-permute-start.12 = (bf16[2,1,16,512]{3,2,1,0:T(8,128)(2,1)S(1)}, bf16[2,1,16,512]{3,2,1,0:T(8,128)(2,1)S(1)}, u32[]{:S(2)}, u32[]{:S(2)}) collective-permute-start(bf16[2,1,16,512]{3,2,1,0:T(8,128)(2,1)S(1)} %get-tuple-element.113), channel_id=1, source_target_pairs={{0,1},{2,3},{4,5},{6,7},{8,9},{10,11},{12,13},{14,15},{16,17},{18,... | collective-permute-start | bytes 98312 | tf_op jit(solution)/shard_map/ppermute | solution.py:32
  9.0 4.5 %collective-permute-start.10 = (bf16[2,8,1,512]{3,2,1,0:T(2,128)(2,1)S(1)}, bf16[2,8,1,512]{3,2,1,0:T(2,128)(2,1)S(1)}, u32[]{:S(2)}, u32[]{:S(2)}) collective-permute-start(bf16[2,8,1,512]{3,2,1,0:T(2,128)(2,1)S(1)} %get-tuple-element.110), channel_id=1, source_target_pairs={{2,0},{4,2},{6,4},{8,6},{10,8},{12,10},{14,12},{16,14},{18,16},{20... | collective-permute-start | bytes 49160 | tf_op jit(solution)/shard_map/ppermute | solution.py:34
  13.6 1.9 %collective-permute-start.9 = (bf16[2,8,1,512]{3,2,1,0:T(2,128)(2,1)S(1)}, bf16[2,8,1,512]{3,2,1,0:T(2,128)(2,1)S(1)}, u32[]{:S(2)}, u32[]{:S(2)}) collective-permute-start(bf16[2,8,1,512]{3,2,1,0:T(2,128)(2,1)S(1)} %get-tuple-element.109), channel_id=1, source_target_pairs={{0,2},{2,4},{4,6},{6,8},{8,10},{10,12},{12,14},{14,16},{16,18},{18... | collective-permute-start | bytes 49160 | tf_op jit(solution)/shard_map/ppermute | solution.py:32
  16.7 3.0 %collective-permute-done.9 = bf16[2,8,1,512]{3,2,1,0:T(2,128)(2,1)S(1)} collective-permute-done((bf16[2,8,1,512]{3,2,1,0:T(2,128)(2,1)S(1)}, bf16[2,8,1,512]{3,2,1,0:T(2,128)(2,1)S(1)}, u32[]{:S(2)}, u32[]{:S(2)}) %collective-permute-start.9) | collective-permute-done | bytes 16416 | tf_op jit(solution)/shard_map/ppermute | solution.py:32
  20.5 3.8 %collective-permute-done.21 = bf16[2,8,2,512]{3,2,1,0:T(2,128)(2,1)S(1)} collective-permute-done((bf16[2,8,2,512]{3,2,1,0:T(2,128)(2,1)S(1)}, bf16[2,8,2,512]{3,2,1,0:T(2,128)(2,1)S(1)}, u32[]{:S(2)}, u32[]{:S(2)}) %collective-permute-start.21) | collective-permute-done | bytes 32800 | tf_op jit(solution)/shard_map/ppermute | solution.py:13
  25.4 3.8 %collective-permute-done.22 = bf16[2,8,4,512]{3,2,1,0:T(4,128)(2,1)S(1)} collective-permute-done((bf16[2,8,4,512]{3,2,1,0:T(4,128)(2,1)S(1)}, bf16[2,8,4,512]{3,2,1,0:T(4,128)(2,1)S(1)}, u32[]{:S(2)}, u32[]{:S(2)}) %collective-permute-start.22) | collective-permute-done | bytes 65568 | tf_op jit(solution)/shard_map/ppermute | solution.py:13
  30.8 3.9 %collective-permute-done.23 = bf16[2,8,8,512]{3,2,1,0:T(8,128)(2,1)S(1)} collective-permute-done((bf16[2,8,8,512]{3,2,1,0:T(8,128)(2,1)S(1)}, bf16[2,8,8,512]{3,2,1,0:T(8,128)(2,1)S(1)}, u32[]{:S(2)}, u32[]{:S(2)}) %collective-permute-start.23) | collective-permute-done | bytes 131104 | tf_op jit(solution)/shard_map/ppermute | solution.py:13
  35.0 2.5 %collective-permute-done.4 = bf16[2,8,16,512]{3,2,1,0:T(8,128)(2,1)S(1)} collective-permute-done((bf16[2,8,16,512]{3,2,1,0:T(8,128)(2,1)S(1)}, bf16[2,8,16,512]{3,2,1,0:T(8,128)(2,1)S(1)}, u32[]{:S(2)}, u32[]{:S(2)}) %collective-permute-start.4) | collective-permute-done | bytes 262176 | tf_op jit(solution)/shard_map/ppermute | solution.py:13
  37.7 3.9 %collective-permute-done.24 = bf16[2,8,16,512]{3,2,1,0:T(8,128)(2,1)S(1)} collective-permute-done((bf16[2,8,16,512]{3,2,1,0:T(8,128)(2,1)S(1)}, bf16[2,8,16,512]{3,2,1,0:T(8,128)(2,1)S(1)}, u32[]{:S(2)}, u32[]{:S(2)}) %collective-permute-start.24) | collective-permute-done | bytes 262176 | tf_op jit(solution)/shard_map/ppermute | solution.py:13
  41.9 5.9 %collective-permute-done.5 = bf16[2,8,16,512]{3,2,1,0:T(8,128)(2,1)S(1)} collective-permute-done((bf16[2,8,16,512]{3,2,1,0:T(8,128)(2,1)S(1)}, bf16[2,8,16,512]{3,2,1,0:T(8,128)(2,1)S(1)}, u32[]{:S(2)}, u32[]{:S(2)}) %collective-permute-start.5) | collective-permute-done | bytes 262176 | tf_op jit(solution)/shard_map/ppermute | solution.py:13
  47.9 1.6 collective-permute-start.6
  49.6 3.9 %collective-permute-done.25 = bf16[2,8,16,512]{3,2,1,0:T(8,128)(2,1)S(1)} collective-permute-done((bf16[2,8,16,512]{3,2,1,0:T(8,128)(2,1)S(1)}, bf16[2,8,16,512]{3,2,1,0:T(8,128)(2,1)S(1)}, u32[]{:S(2)}, u32[]{:S(2)}) %collective-permute-start.25) | collective-permute-done | bytes 262176 | tf_op jit(solution)/shard_map/ppermute | solution.py:13
  53.6 1.6 collective-permute-start.26
  55.2 8.4 %collective-permute-done.6 = bf16[2,8,16,512]{3,2,1,0:T(8,128)(2,1)S(1)} collective-permute-done((bf16[2,8,16,512]{3,2,1,0:T(8,128)(2,1)S(1)}, bf16[2,8,16,512]{3,2,1,0:T(8,128)(2,1)S(1)}, u32[]{:S(2)}, u32[]{:S(2)}) %collective-permute-start.6) | collective-permute-done | bytes 262176 | tf_op jit(solution)/shard_map/ppermute | solution.py:13
  63.7 2.0 %collective-permute-start.7 = (bf16[2,8,16,512]{3,2,1,0:T(8,128)(2,1)S(1)}, bf16[2,8,16,512]{3,2,1,0:T(8,128)(2,1)S(1)}, u32[]{:S(2)}, u32[]{:S(2)}) collective-permute-start(bf16[2,8,16,512]{3,2,1,0:T(8,128)(2,1)S(1)} %broadcast_select_fusion.8), channel_id=1, source_target_pairs={{0,16},{2,18},{4,20},{6,22},{8,24},{10,26},{12,28},{14,30},{16,0},... | collective-permute-start | bytes 786440 | tf_op jit(solution)/shard_map/ppermute | solution.py:13
  65.7 3.5 %collective-permute-done.26 = bf16[2,8,16,512]{3,2,1,0:T(8,128)(2,1)S(1)} collective-permute-done((bf16[2,8,16,512]{3,2,1,0:T(8,128)(2,1)S(1)}, bf16[2,8,16,512]{3,2,1,0:T(8,128)(2,1)S(1)}, u32[]{:S(2)}, u32[]{:S(2)}) %collective-permute-start.26) | collective-permute-done | bytes 262176 | tf_op jit(solution)/shard_map/ppermute | solution.py:13
  69.3 2.0 %collective-permute-start.27 = (bf16[2,8,16,512]{3,2,1,0:T(8,128)(2,1)S(1)}, bf16[2,8,16,512]{3,2,1,0:T(8,128)(2,1)S(1)}, u32[]{:S(2)}, u32[]{:S(2)}) collective-permute-start(bf16[2,8,16,512]{3,2,1,0:T(8,128)(2,1)S(1)} %broadcast_select_fusion.3), channel_id=1, source_target_pairs={{0,16},{2,18},{4,20},{6,22},{8,24},{10,26},{12,28},{14,30},{16,0},... | collective-permute-start | bytes 786440 | tf_op jit(solution)/shard_map/ppermute | solution.py:13
  71.4 7.9 %collective-permute-done.7 = bf16[2,8,16,512]{3,2,1,0:T(8,128)(2,1)S(1)} collective-permute-done((bf16[2,8,16,512]{3,2,1,0:T(8,128)(2,1)S(1)}, bf16[2,8,16,512]{3,2,1,0:T(8,128)(2,1)S(1)}, u32[]{:S(2)}, u32[]{:S(2)}) %collective-permute-start.7) | collective-permute-done | bytes 262176 | tf_op jit(solution)/shard_map/ppermute | solution.py:13
  79.5 2.8 %collective-permute-done.27 = bf16[2,8,16,512]{3,2,1,0:T(8,128)(2,1)S(1)} collective-permute-done((bf16[2,8,16,512]{3,2,1,0:T(8,128)(2,1)S(1)}, bf16[2,8,16,512]{3,2,1,0:T(8,128)(2,1)S(1)}, u32[]{:S(2)}, u32[]{:S(2)}) %collective-permute-start.27) | collective-permute-done | bytes 262176 | tf_op jit(solution)/shard_map/ppermute | solution.py:13
  82.5 5.2 %collective-permute-done.8 = bf16[2,8,1,512]{3,2,1,0:T(2,128)(2,1)S(1)} collective-permute-done((bf16[2,8,1,512]{3,2,1,0:T(2,128)(2,1)S(1)}, bf16[2,8,1,512]{3,2,1,0:T(2,128)(2,1)S(1)}, u32[]{:S(2)}, u32[]{:S(2)}) %collective-permute-start.8) | collective-permute-done | bytes 16416 | tf_op jit(solution)/shard_map/ppermute | solution.py:13
  89.3 1.3 collective-permute-start.15
  90.6 4.5 %collective-permute-start.16 = (bf16[2,1,16,512]{3,2,1,0:T(8,128)(2,1)S(1)}, bf16[2,1,16,512]{3,2,1,0:T(8,128)(2,1)S(1)}, u32[]{:S(2)}, u32[]{:S(2)}) collective-permute-start(bf16[2,1,16,512]{3,2,1,0:T(8,128)(2,1)S(1)} %get-tuple-element.107), channel_id=1, source_target_pairs={{0,1},{2,3},{4,5},{6,7},{8,9},{10,11},{12,13},{14,15},{16,17},{18,... | collective-permute-start | bytes 98312 | tf_op jit(solution)/shard_map/ppermute | solution.py:32
  95.3 5.7 %collective-permute-start.14 = (bf16[2,8,1,512]{3,2,1,0:T(2,128)(2,1)S(1)}, bf16[2,8,1,512]{3,2,1,0:T(2,128)(2,1)S(1)}, u32[]{:S(2)}, u32[]{:S(2)}) collective-permute-start(bf16[2,8,1,512]{3,2,1,0:T(2,128)(2,1)S(1)} %get-tuple-element.106), channel_id=1, source_target_pairs={{2,0},{4,2},{6,4},{8,6},{10,8},{12,10},{14,12},{16,14},{18,16},{20... | collective-permute-start | bytes 49160 | tf_op jit(solution)/shard_map/ppermute | solution.py:34
  101.0 1.9 %collective-permute-start.13 = (bf16[2,8,1,512]{3,2,1,0:T(2,128)(2,1)S(1)}, bf16[2,8,1,512]{3,2,1,0:T(2,128)(2,1)S(1)}, u32[]{:S(2)}, u32[]{:S(2)}) collective-permute-start(bf16[2,8,1,512]{3,2,1,0:T(2,128)(2,1)S(1)} %get-tuple-element.105), channel_id=1, source_target_pairs={{0,2},{2,4},{4,6},{6,8},{8,10},{10,12},{12,14},{14,16},{16,18},{18... | collective-permute-start | bytes 49160 | tf_op jit(solution)/shard_map/ppermute | solution.py:32
  103.2 3.9 %collective-permute-done.13 = bf16[2,8,1,512]{3,2,1,0:T(2,128)(2,1)S(1)} collective-permute-done((bf16[2,8,1,512]{3,2,1,0:T(2,128)(2,1)S(1)}, bf16[2,8,1,512]{3,2,1,0:T(2,128)(2,1)S(1)}, u32[]{:S(2)}, u32[]{:S(2)}) %collective-permute-start.13) | collective-permute-done | bytes 16416 | tf_op jit(solution)/shard_map/ppermute | solution.py:32
  109.0 1.3 collective-permute-start.19
  110.3 4.5 %collective-permute-start.20 = (bf16[2,1,16,512]{3,2,1,0:T(8,128)(2,1)S(1)}, bf16[2,1,16,512]{3,2,1,0:T(8,128)(2,1)S(1)}, u32[]{:S(2)}, u32[]{:S(2)}) collective-permute-start(bf16[2,1,16,512]{3,2,1,0:T(8,128)(2,1)S(1)} %get-tuple-element.103), channel_id=1, source_target_pairs={{0,1},{2,3},{4,5},{6,7},{8,9},{10,11},{12,13},{14,15},{16,17},{18,... | collective-permute-start | bytes 98312 | tf_op jit(solution)/shard_map/ppermute | solution.py:32
  115.0 1.9 %collective-permute-start.18 = (bf16[2,8,1,512]{3,2,1,0:T(2,128)(2,1)S(1)}, bf16[2,8,1,512]{3,2,1,0:T(2,128)(2,1)S(1)}, u32[]{:S(2)}, u32[]{:S(2)}) collective-permute-start(bf16[2,8,1,512]{3,2,1,0:T(2,128)(2,1)S(1)} %get-tuple-element.102), channel_id=1, source_target_pairs={{2,0},{4,2},{6,4},{8,6},{10,8},{12,10},{14,12},{16,14},{18,16},{20... | collective-permute-start | bytes 49160 | tf_op jit(solution)/shard_map/ppermute | solution.py:34
  116.9 2.4 %collective-permute-start.17 = (bf16[2,8,1,512]{3,2,1,0:T(2,128)(2,1)S(1)}, bf16[2,8,1,512]{3,2,1,0:T(2,128)(2,1)S(1)}, u32[]{:S(2)}, u32[]{:S(2)}) collective-permute-start(bf16[2,8,1,512]{3,2,1,0:T(2,128)(2,1)S(1)} %get-tuple-element.101), channel_id=1, source_target_pairs={{0,2},{2,4},{4,6},{6,8},{8,10},{10,12},{12,14},{14,16},{16,18},{18... | collective-permute-start | bytes 49160 | tf_op jit(solution)/shard_map/ppermute | solution.py:32
  119.4 3.6 %collective-permute-done.17 = bf16[2,8,1,512]{3,2,1,0:T(2,128)(2,1)S(1)} collective-permute-done((bf16[2,8,1,512]{3,2,1,0:T(2,128)(2,1)S(1)}, bf16[2,8,1,512]{3,2,1,0:T(2,128)(2,1)S(1)}, u32[]{:S(2)}, u32[]{:S(2)}) %collective-permute-start.17) | collective-permute-done | bytes 16416 | tf_op jit(solution)/shard_map/ppermute | solution.py:32
  125.2 1.3 collective-permute-start.31
  126.5 4.5 %collective-permute-start.32 = (bf16[2,1,16,512]{3,2,1,0:T(8,128)(2,1)S(1)}, bf16[2,1,16,512]{3,2,1,0:T(8,128)(2,1)S(1)}, u32[]{:S(2)}, u32[]{:S(2)}) collective-permute-start(bf16[2,1,16,512]{3,2,1,0:T(8,128)(2,1)S(1)} %get-tuple-element.99), channel_id=1, source_target_pairs={{0,1},{2,3},{4,5},{6,7},{8,9},{10,11},{12,13},{14,15},{16,17},{18,... | collective-permute-start | bytes 98312 | tf_op jit(solution)/shard_map/ppermute | solution.py:32
  131.1 1.9 %collective-permute-start.30 = (bf16[2,8,1,512]{3,2,1,0:T(2,128)(2,1)S(1)}, bf16[2,8,1,512]{3,2,1,0:T(2,128)(2,1)S(1)}, u32[]{:S(2)}, u32[]{:S(2)}) collective-permute-start(bf16[2,8,1,512]{3,2,1,0:T(2,128)(2,1)S(1)} %get-tuple-element.96), channel_id=1, source_target_pairs={{2,0},{4,2},{6,4},{8,6},{10,8},{12,10},{14,12},{16,14},{18,16},{20... | collective-permute-start | bytes 49160 | tf_op jit(solution)/shard_map/ppermute | solution.py:34
  133.0 2.6 %collective-permute-start.29 = (bf16[2,8,1,512]{3,2,1,0:T(2,128)(2,1)S(1)}, bf16[2,8,1,512]{3,2,1,0:T(2,128)(2,1)S(1)}, u32[]{:S(2)}, u32[]{:S(2)}) collective-permute-start(bf16[2,8,1,512]{3,2,1,0:T(2,128)(2,1)S(1)} %get-tuple-element.95), channel_id=1, source_target_pairs={{0,2},{2,4},{4,6},{6,8},{8,10},{10,12},{12,14},{14,16},{16,18},{18... | collective-permute-start | bytes 49160 | tf_op jit(solution)/shard_map/ppermute | solution.py:32
  135.7 3.4 %collective-permute-done.29 = bf16[2,8,1,512]{3,2,1,0:T(2,128)(2,1)S(1)} collective-permute-done((bf16[2,8,1,512]{3,2,1,0:T(2,128)(2,1)S(1)}, bf16[2,8,1,512]{3,2,1,0:T(2,128)(2,1)S(1)}, u32[]{:S(2)}, u32[]{:S(2)}) %collective-permute-start.29) | collective-permute-done | bytes 16416 | tf_op jit(solution)/shard_map/ppermute | solution.py:32
  140.9 1.3 collective-permute-start.35
  142.2 4.5 %collective-permute-start.36 = (bf16[2,1,16,512]{3,2,1,0:T(8,128)(2,1)S(1)}, bf16[2,1,16,512]{3,2,1,0:T(8,128)(2,1)S(1)}, u32[]{:S(2)}, u32[]{:S(2)}) collective-permute-start(bf16[2,1,16,512]{3,2,1,0:T(8,128)(2,1)S(1)} %get-tuple-element.93), channel_id=1, source_target_pairs={{0,1},{2,3},{4,5},{6,7},{8,9},{10,11},{12,13},{14,15},{16,17},{18,... | collective-permute-start | bytes 98312 | tf_op jit(solution)/shard_map/ppermute | solution.py:32
  146.8 1.9 %collective-permute-start.34 = (bf16[2,8,1,512]{3,2,1,0:T(2,128)(2,1)S(1)}, bf16[2,8,1,512]{3,2,1,0:T(2,128)(2,1)S(1)}, u32[]{:S(2)}, u32[]{:S(2)}) collective-permute-start(bf16[2,8,1,512]{3,2,1,0:T(2,128)(2,1)S(1)} %get-tuple-element.92), channel_id=1, source_target_pairs={{2,0},{4,2},{6,4},{8,6},{10,8},{12,10},{14,12},{16,14},{18,16},{20... | collective-permute-start | bytes 49160 | tf_op jit(solution)/shard_map/ppermute | solution.py:34
  148.7 2.4 %collective-permute-start.33 = (bf16[2,8,1,512]{3,2,1,0:T(2,128)(2,1)S(1)}, bf16[2,8,1,512]{3,2,1,0:T(2,128)(2,1)S(1)}, u32[]{:S(2)}, u32[]{:S(2)}) collective-permute-start(bf16[2,8,1,512]{3,2,1,0:T(2,128)(2,1)S(1)} %get-tuple-element.91), channel_id=1, source_target_pairs={{0,2},{2,4},{4,6},{6,8},{8,10},{10,12},{12,14},{14,16},{16,18},{18... | collective-permute-start | bytes 49160 | tf_op jit(solution)/shard_map/ppermute | solution.py:32
  151.3 3.6 %collective-permute-done.33 = bf16[2,8,1,512]{3,2,1,0:T(2,128)(2,1)S(1)} collective-permute-done((bf16[2,8,1,512]{3,2,1,0:T(2,128)(2,1)S(1)}, bf16[2,8,1,512]{3,2,1,0:T(2,128)(2,1)S(1)}, u32[]{:S(2)}, u32[]{:S(2)}) %collective-permute-start.33) | collective-permute-done | bytes 16416 | tf_op jit(solution)/shard_map/ppermute | solution.py:32
  156.8 1.3 collective-permute-start.39
  158.1 4.5 %collective-permute-start.40 = (bf16[2,1,16,512]{3,2,1,0:T(8,128)(2,1)S(1)}, bf16[2,1,16,512]{3,2,1,0:T(8,128)(2,1)S(1)}, u32[]{:S(2)}, u32[]{:S(2)}) collective-permute-start(bf16[2,1,16,512]{3,2,1,0:T(8,128)(2,1)S(1)} %get-tuple-element.89), channel_id=1, source_target_pairs={{0,1},{2,3},{4,5},{6,7},{8,9},{10,11},{12,13},{14,15},{16,17},{18,... | collective-permute-start | bytes 98312 | tf_op jit(solution)/shard_map/ppermute | solution.py:32
  162.7 1.9 %collective-permute-start.38 = (bf16[2,8,1,512]{3,2,1,0:T(2,128)(2,1)S(1)}, bf16[2,8,1,512]{3,2,1,0:T(2,128)(2,1)S(1)}, u32[]{:S(2)}, u32[]{:S(2)}) collective-permute-start(bf16[2,8,1,512]{3,2,1,0:T(2,128)(2,1)S(1)} %get-tuple-element.88), channel_id=1, source_target_pairs={{2,0},{4,2},{6,4},{8,6},{10,8},{12,10},{14,12},{16,14},{18,16},{20... | collective-permute-start | bytes 49160 | tf_op jit(solution)/shard_map/ppermute | solution.py:34
  164.6 2.4 %collective-permute-start.37 = (bf16[2,8,1,512]{3,2,1,0:T(2,128)(2,1)S(1)}, bf16[2,8,1,512]{3,2,1,0:T(2,128)(2,1)S(1)}, u32[]{:S(2)}, u32[]{:S(2)}) collective-permute-start(bf16[2,8,1,512]{3,2,1,0:T(2,128)(2,1)S(1)} %get-tuple-element.87), channel_id=1, source_target_pairs={{0,2},{2,4},{4,6},{6,8},{8,10},{10,12},{12,14},{14,16},{16,18},{18... | collective-permute-start | bytes 49160 | tf_op jit(solution)/shard_map/ppermute | solution.py:32
  167.2 3.6 %collective-permute-done.37 = bf16[2,8,1,512]{3,2,1,0:T(2,128)(2,1)S(1)} collective-permute-done((bf16[2,8,1,512]{3,2,1,0:T(2,128)(2,1)S(1)}, bf16[2,8,1,512]{3,2,1,0:T(2,128)(2,1)S(1)}, u32[]{:S(2)}, u32[]{:S(2)}) %collective-permute-start.37) | collective-permute-done | bytes 16416 | tf_op jit(solution)/shard_map/ppermute | solution.py:32
  171.6 1.5 fusion.19
  (161 shorter events, 16.9 us)
Async XLA Ops:
  0.0 2.9 %copy-start = (f32[4,8,16,512]{3,2,1,0:T(8,128)S(1)}, f32[4,8,16,512]{3,2,1,0:T(8,128)}, u32[]{:S(2)}) copy-start(f32[4,8,16,512]{3,2,1,0:T(8,128)} %param.7) | copy-start | bytes 3145732
  2.9 6.0 %copy-start.1 = (bf16[2,8,16,512]{3,2,1,0:T(8,128)(2,1)S(1)}, bf16[2,8,16,512]{3,2,1,0:T(8,128)(2,1)}, u32[]{:S(2)}) copy-start(bf16[2,8,16,512]{3,2,1,0:T(8,128)(2,1)} %param.8) | copy-start | bytes 786436
  2.9 12.6 %copy-start.6 = (s32[2,8]{1,0:T(2,128)S(1)}, s32[2,8]{1,0:T(2,128)}, u32[]{:S(2)}) copy-start(s32[2,8]{1,0:T(2,128)} %param.12) | copy-start | bytes 196
  2.9 12.7 %copy-start.5 = (s32[2,8]{1,0:T(2,128)S(1)}, s32[2,8]{1,0:T(2,128)}, u32[]{:S(2)}) copy-start(s32[2,8]{1,0:T(2,128)} %param.13) | copy-start | bytes 196
  3.0 31.9 %collective-permute-start.11 = (bf16[2,1,16,512]{3,2,1,0:T(8,128)(2,1)S(1)}, bf16[2,1,16,512]{3,2,1,0:T(8,128)(2,1)S(1)}, u32[]{:S(2)}, u32[]{:S(2)}) collective-permute-start(bf16[2,1,16,512]{3,2,1,0:T(8,128)(2,1)S(1)} %get-tuple-element.114), channel_id=1, source_target_pairs={{1,0},{3,2},{5,4},{7,6},{9,8},{11,10},{13,12},{15,14},{17,16},{19,... | collective-permute-start | bytes 98312 | tf_op jit(solution)/shard_map/ppermute | solution.py:34
  4.3 50.9 %collective-permute-start.12 = (bf16[2,1,16,512]{3,2,1,0:T(8,128)(2,1)S(1)}, bf16[2,1,16,512]{3,2,1,0:T(8,128)(2,1)S(1)}, u32[]{:S(2)}, u32[]{:S(2)}) collective-permute-start(bf16[2,1,16,512]{3,2,1,0:T(8,128)(2,1)S(1)} %get-tuple-element.113), channel_id=1, source_target_pairs={{0,1},{2,3},{4,5},{6,7},{8,9},{10,11},{12,13},{14,15},{16,17},{18,... | collective-permute-start | bytes 98312 | tf_op jit(solution)/shard_map/ppermute | solution.py:32
  8.9 6.7 %collective-permute-start = (bf16[2,8,1,512]{3,2,1,0:T(2,128)(2,1)S(1)}, bf16[2,8,1,512]{3,2,1,0:T(2,128)(2,1)S(1)}, u32[]{:S(2)}, u32[]{:S(2)}) collective-permute-start(bf16[2,8,1,512]{3,2,1,0:T(2,128)(2,1)S(1)} %slice.780), channel_id=1, source_target_pairs={{0,2},{2,4},{4,6},{6,8},{8,10},{10,12},{12,14},{14,16},{16,18},{18... | collective-permute-start | bytes 49160 | tf_op jit(solution)/shard_map/ppermute | solution.py:13
  9.0 7.6 %collective-permute-start.10 = (bf16[2,8,1,512]{3,2,1,0:T(2,128)(2,1)S(1)}, bf16[2,8,1,512]{3,2,1,0:T(2,128)(2,1)S(1)}, u32[]{:S(2)}, u32[]{:S(2)}) collective-permute-start(bf16[2,8,1,512]{3,2,1,0:T(2,128)(2,1)S(1)} %get-tuple-element.110), channel_id=1, source_target_pairs={{2,0},{4,2},{6,4},{8,6},{10,8},{12,10},{14,12},{16,14},{18,16},{20... | collective-permute-start | bytes 49160 | tf_op jit(solution)/shard_map/ppermute | solution.py:34
  13.6 6.1 %collective-permute-start.9 = (bf16[2,8,1,512]{3,2,1,0:T(2,128)(2,1)S(1)}, bf16[2,8,1,512]{3,2,1,0:T(2,128)(2,1)S(1)}, u32[]{:S(2)}, u32[]{:S(2)}) collective-permute-start(bf16[2,8,1,512]{3,2,1,0:T(2,128)(2,1)S(1)} %get-tuple-element.109), channel_id=1, source_target_pairs={{0,2},{2,4},{4,6},{6,8},{8,10},{10,12},{12,14},{14,16},{16,18},{18... | collective-permute-start | bytes 49160 | tf_op jit(solution)/shard_map/ppermute | solution.py:32
  15.9 4.3 %collective-permute-start.1 = (bf16[2,8,2,512]{3,2,1,0:T(2,128)(2,1)S(1)}, bf16[2,8,2,512]{3,2,1,0:T(2,128)(2,1)S(1)}, u32[]{:S(2)}, u32[]{:S(2)}) collective-permute-start(bf16[2,8,2,512]{3,2,1,0:T(2,128)(2,1)S(1)} %slice.990), channel_id=1, source_target_pairs={{0,2},{2,4},{4,6},{6,8},{8,10},{10,12},{12,14},{14,16},{16,18},{18... | collective-permute-start | bytes 98312 | tf_op jit(solution)/shard_map/ppermute | solution.py:13
  20.0 4.3 %collective-permute-start.21 = (bf16[2,8,2,512]{3,2,1,0:T(2,128)(2,1)S(1)}, bf16[2,8,2,512]{3,2,1,0:T(2,128)(2,1)S(1)}, u32[]{:S(2)}, u32[]{:S(2)}) collective-permute-start(bf16[2,8,2,512]{3,2,1,0:T(2,128)(2,1)S(1)} %slice.1072), channel_id=1, source_target_pairs={{0,2},{2,4},{4,6},{6,8},{8,10},{10,12},{12,14},{14,16},{16,18},{18... | collective-permute-start | bytes 98312 | tf_op jit(solution)/shard_map/ppermute | solution.py:13
  20.4 4.6 %collective-permute-start.2 = (bf16[2,8,4,512]{3,2,1,0:T(4,128)(2,1)S(1)}, bf16[2,8,4,512]{3,2,1,0:T(4,128)(2,1)S(1)}, u32[]{:S(2)}, u32[]{:S(2)}) collective-permute-start(bf16[2,8,4,512]{3,2,1,0:T(4,128)(2,1)S(1)} %slice.992), channel_id=1, source_target_pairs={{0,2},{2,4},{4,6},{6,8},{8,10},{10,12},{12,14},{14,16},{16,18},{18... | collective-permute-start | bytes 196616 | tf_op jit(solution)/shard_map/ppermute | solution.py:13
  24.5 4.6 %collective-permute-start.22 = (bf16[2,8,4,512]{3,2,1,0:T(4,128)(2,1)S(1)}, bf16[2,8,4,512]{3,2,1,0:T(4,128)(2,1)S(1)}, u32[]{:S(2)}, u32[]{:S(2)}) collective-permute-start(bf16[2,8,4,512]{3,2,1,0:T(4,128)(2,1)S(1)} %slice.1074), channel_id=1, source_target_pairs={{0,2},{2,4},{4,6},{6,8},{8,10},{10,12},{12,14},{14,16},{16,18},{18... | collective-permute-start | bytes 196616 | tf_op jit(solution)/shard_map/ppermute | solution.py:13
  25.3 5.3 %collective-permute-start.3 = (bf16[2,8,8,512]{3,2,1,0:T(8,128)(2,1)S(1)}, bf16[2,8,8,512]{3,2,1,0:T(8,128)(2,1)S(1)}, u32[]{:S(2)}, u32[]{:S(2)}) collective-permute-start(bf16[2,8,8,512]{3,2,1,0:T(8,128)(2,1)S(1)} %get-tuple-element.111), channel_id=1, source_target_pairs={{0,2},{2,4},{4,6},{6,8},{8,10},{10,12},{12,14},{14,16},{16,18},{18... | collective-permute-start | bytes 393224 | tf_op jit(solution)/shard_map/ppermute | solution.py:13
  29.4 5.3 %collective-permute-start.23 = (bf16[2,8,8,512]{3,2,1,0:T(8,128)(2,1)S(1)}, bf16[2,8,8,512]{3,2,1,0:T(8,128)(2,1)S(1)}, u32[]{:S(2)}, u32[]{:S(2)}) collective-permute-start(bf16[2,8,8,512]{3,2,1,0:T(8,128)(2,1)S(1)} %get-tuple-element.97), channel_id=1, source_target_pairs={{0,2},{2,4},{4,6},{6,8},{8,10},{10,12},{12,14},{14,16},{16,18},{18... | collective-permute-start | bytes 393224 | tf_op jit(solution)/shard_map/ppermute | solution.py:13
  30.8 6.8 %collective-permute-start.4 = (bf16[2,8,16,512]{3,2,1,0:T(8,128)(2,1)S(1)}, bf16[2,8,16,512]{3,2,1,0:T(8,128)(2,1)S(1)}, u32[]{:S(2)}, u32[]{:S(2)}) collective-permute-start(bf16[2,8,16,512]{3,2,1,0:T(8,128)(2,1)S(1)} %maximum_select_fusion.2), channel_id=1, source_target_pairs={{0,2},{2,4},{4,6},{6,8},{8,10},{10,12},{12,14},{14,16},{16,18},{18... | collective-permute-start | bytes 786440 | tf_op jit(solution)/shard_map/ppermute | solution.py:13
  34.9 6.7 %collective-permute-start.24 = (bf16[2,8,16,512]{3,2,1,0:T(8,128)(2,1)S(1)}, bf16[2,8,16,512]{3,2,1,0:T(8,128)(2,1)S(1)}, u32[]{:S(2)}, u32[]{:S(2)}) collective-permute-start(bf16[2,8,16,512]{3,2,1,0:T(8,128)(2,1)S(1)} %maximum_select_fusion.5), channel_id=1, source_target_pairs={{0,2},{2,4},{4,6},{6,8},{8,10},{10,12},{12,14},{14,16},{16,18},{18... | collective-permute-start | bytes 786440 | tf_op jit(solution)/shard_map/ppermute | solution.py:13
  37.7 10.2 %collective-permute-start.5 = (bf16[2,8,16,512]{3,2,1,0:T(8,128)(2,1)S(1)}, bf16[2,8,16,512]{3,2,1,0:T(8,128)(2,1)S(1)}, u32[]{:S(2)}, u32[]{:S(2)}) collective-permute-start(bf16[2,8,16,512]{3,2,1,0:T(8,128)(2,1)S(1)} %broadcast_select_fusion.6), channel_id=1, source_target_pairs={{0,4},{2,6},{4,8},{6,10},{8,12},{10,14},{12,16},{14,18},{16,20},{1... | collective-permute-start | bytes 786440 | tf_op jit(solution)/shard_map/ppermute | solution.py:13
  41.7 11.7 %collective-permute-start.25 = (bf16[2,8,16,512]{3,2,1,0:T(8,128)(2,1)S(1)}, bf16[2,8,16,512]{3,2,1,0:T(8,128)(2,1)S(1)}, u32[]{:S(2)}, u32[]{:S(2)}) collective-permute-start(bf16[2,8,16,512]{3,2,1,0:T(8,128)(2,1)S(1)} %broadcast_select_fusion.1), channel_id=1, source_target_pairs={{0,4},{2,6},{4,8},{6,10},{8,12},{10,14},{12,16},{14,18},{16,20},{1... | collective-permute-start | bytes 786440 | tf_op jit(solution)/shard_map/ppermute | solution.py:13
  41.9 13.3 %copy-start.3 = (s32[16,512]{1,0:T(8,128)S(1)}, s32[16,512]{1,0:T(8,128)}, u32[]{:S(2)}) copy-start(s32[16,512]{1,0:T(8,128)} %param.11) | copy-start | bytes 98308
  41.9 13.3 %copy-start.4 = (f32[16,512]{1,0:T(8,128)S(1)}, f32[16,512]{1,0:T(8,128)}, u32[]{:S(2)}) copy-start(f32[16,512]{1,0:T(8,128)} %param.10) | copy-start | bytes 98308
  47.9 15.7 %collective-permute-start.6 = (bf16[2,8,16,512]{3,2,1,0:T(8,128)(2,1)S(1)}, bf16[2,8,16,512]{3,2,1,0:T(8,128)(2,1)S(1)}, u32[]{:S(2)}, u32[]{:S(2)}) collective-permute-start(bf16[2,8,16,512]{3,2,1,0:T(8,128)(2,1)S(1)} %broadcast_select_fusion.7), channel_id=1, source_target_pairs={{0,8},{2,10},{4,12},{6,14},{8,16},{10,18},{12,20},{14,22},{16,24},... | collective-permute-start | bytes 786440 | tf_op jit(solution)/shard_map/ppermute | solution.py:13
  53.6 15.7 %collective-permute-start.26 = (bf16[2,8,16,512]{3,2,1,0:T(8,128)(2,1)S(1)}, bf16[2,8,16,512]{3,2,1,0:T(8,128)(2,1)S(1)}, u32[]{:S(2)}, u32[]{:S(2)}) collective-permute-start(bf16[2,8,16,512]{3,2,1,0:T(8,128)(2,1)S(1)} %broadcast_select_fusion.2), channel_id=1, source_target_pairs={{0,8},{2,10},{4,12},{6,14},{8,16},{10,18},{12,20},{14,22},{16,24},... | collective-permute-start | bytes 786440 | tf_op jit(solution)/shard_map/ppermute | solution.py:13
  63.7 15.5 %collective-permute-start.7 = (bf16[2,8,16,512]{3,2,1,0:T(8,128)(2,1)S(1)}, bf16[2,8,16,512]{3,2,1,0:T(8,128)(2,1)S(1)}, u32[]{:S(2)}, u32[]{:S(2)}) collective-permute-start(bf16[2,8,16,512]{3,2,1,0:T(8,128)(2,1)S(1)} %broadcast_select_fusion.8), channel_id=1, source_target_pairs={{0,16},{2,18},{4,20},{6,22},{8,24},{10,26},{12,28},{14,30},{16,0},... | collective-permute-start | bytes 786440 | tf_op jit(solution)/shard_map/ppermute | solution.py:13
  69.3 12.9 %collective-permute-start.27 = (bf16[2,8,16,512]{3,2,1,0:T(8,128)(2,1)S(1)}, bf16[2,8,16,512]{3,2,1,0:T(8,128)(2,1)S(1)}, u32[]{:S(2)}, u32[]{:S(2)}) collective-permute-start(bf16[2,8,16,512]{3,2,1,0:T(8,128)(2,1)S(1)} %broadcast_select_fusion.3), channel_id=1, source_target_pairs={{0,16},{2,18},{4,20},{6,22},{8,24},{10,26},{12,28},{14,30},{16,0},... | collective-permute-start | bytes 786440 | tf_op jit(solution)/shard_map/ppermute | solution.py:13
  79.4 8.5 %copy-start.2 = (f32[8]{0:T(128)S(1)}, f32[8]{0:T(128)}, u32[]{:S(2)}) copy-start(f32[8]{0:T(128)} %param.9) | copy-start | bytes 100
  79.4 8.3 %collective-permute-start.8 = (bf16[2,8,1,512]{3,2,1,0:T(2,128)(2,1)S(1)}, bf16[2,8,1,512]{3,2,1,0:T(2,128)(2,1)S(1)}, u32[]{:S(2)}, u32[]{:S(2)}) collective-permute-start(bf16[2,8,1,512]{3,2,1,0:T(2,128)(2,1)S(1)} %slice.996), channel_id=1, source_target_pairs={{0,2},{2,4},{4,6},{6,8},{8,10},{10,12},{12,14},{14,16},{16,18},{18... | collective-permute-start | bytes 49160 | tf_op jit(solution)/shard_map/ppermute | solution.py:13
  82.4 20.5 %collective-permute-start.28 = (bf16[2,8,1,512]{3,2,1,0:T(2,128)(2,1)S(1)}, bf16[2,8,1,512]{3,2,1,0:T(2,128)(2,1)S(1)}, u32[]{:S(2)}, u32[]{:S(2)}) collective-permute-start(bf16[2,8,1,512]{3,2,1,0:T(2,128)(2,1)S(1)} %slice.1078), channel_id=1, source_target_pairs={{0,2},{2,4},{4,6},{6,8},{8,10},{10,12},{12,14},{14,16},{16,18},{18... | collective-permute-start | bytes 49160 | tf_op jit(solution)/shard_map/ppermute | solution.py:13
  89.3 18.0 %collective-permute-start.15 = (bf16[2,1,16,512]{3,2,1,0:T(8,128)(2,1)S(1)}, bf16[2,1,16,512]{3,2,1,0:T(8,128)(2,1)S(1)}, u32[]{:S(2)}, u32[]{:S(2)}) collective-permute-start(bf16[2,1,16,512]{3,2,1,0:T(8,128)(2,1)S(1)} %get-tuple-element.108), channel_id=1, source_target_pairs={{1,0},{3,2},{5,4},{7,6},{9,8},{11,10},{13,12},{15,14},{17,16},{19,... | collective-permute-start | bytes 98312 | tf_op jit(solution)/shard_map/ppermute | solution.py:34
  90.6 16.9 %collective-permute-start.16 = (bf16[2,1,16,512]{3,2,1,0:T(8,128)(2,1)S(1)}, bf16[2,1,16,512]{3,2,1,0:T(8,128)(2,1)S(1)}, u32[]{:S(2)}, u32[]{:S(2)}) collective-permute-start(bf16[2,1,16,512]{3,2,1,0:T(8,128)(2,1)S(1)} %get-tuple-element.107), channel_id=1, source_target_pairs={{0,1},{2,3},{4,5},{6,7},{8,9},{10,11},{12,13},{14,15},{16,17},{18,... | collective-permute-start | bytes 98312 | tf_op jit(solution)/shard_map/ppermute | solution.py:32
  95.3 8.0 %collective-permute-start.14 = (bf16[2,8,1,512]{3,2,1,0:T(2,128)(2,1)S(1)}, bf16[2,8,1,512]{3,2,1,0:T(2,128)(2,1)S(1)}, u32[]{:S(2)}, u32[]{:S(2)}) collective-permute-start(bf16[2,8,1,512]{3,2,1,0:T(2,128)(2,1)S(1)} %get-tuple-element.106), channel_id=1, source_target_pairs={{2,0},{4,2},{6,4},{8,6},{10,8},{12,10},{14,12},{16,14},{18,16},{20... | collective-permute-start | bytes 49160 | tf_op jit(solution)/shard_map/ppermute | solution.py:34
  101.0 6.1 %collective-permute-start.13 = (bf16[2,8,1,512]{3,2,1,0:T(2,128)(2,1)S(1)}, bf16[2,8,1,512]{3,2,1,0:T(2,128)(2,1)S(1)}, u32[]{:S(2)}, u32[]{:S(2)}) collective-permute-start(bf16[2,8,1,512]{3,2,1,0:T(2,128)(2,1)S(1)} %get-tuple-element.105), channel_id=1, source_target_pairs={{0,2},{2,4},{4,6},{6,8},{8,10},{10,12},{12,14},{14,16},{16,18},{18... | collective-permute-start | bytes 49160 | tf_op jit(solution)/shard_map/ppermute | solution.py:32
  109.0 14.2 %collective-permute-start.19 = (bf16[2,1,16,512]{3,2,1,0:T(8,128)(2,1)S(1)}, bf16[2,1,16,512]{3,2,1,0:T(8,128)(2,1)S(1)}, u32[]{:S(2)}, u32[]{:S(2)}) collective-permute-start(bf16[2,1,16,512]{3,2,1,0:T(8,128)(2,1)S(1)} %get-tuple-element.104), channel_id=1, source_target_pairs={{1,0},{3,2},{5,4},{7,6},{9,8},{11,10},{13,12},{15,14},{17,16},{19,... | collective-permute-start | bytes 98312 | tf_op jit(solution)/shard_map/ppermute | solution.py:34
  110.3 13.1 %collective-permute-start.20 = (bf16[2,1,16,512]{3,2,1,0:T(8,128)(2,1)S(1)}, bf16[2,1,16,512]{3,2,1,0:T(8,128)(2,1)S(1)}, u32[]{:S(2)}, u32[]{:S(2)}) collective-permute-start(bf16[2,1,16,512]{3,2,1,0:T(8,128)(2,1)S(1)} %get-tuple-element.103), channel_id=1, source_target_pairs={{0,1},{2,3},{4,5},{6,7},{8,9},{10,11},{12,13},{14,15},{16,17},{18,... | collective-permute-start | bytes 98312 | tf_op jit(solution)/shard_map/ppermute | solution.py:32
  115.0 4.5 %collective-permute-start.18 = (bf16[2,8,1,512]{3,2,1,0:T(2,128)(2,1)S(1)}, bf16[2,8,1,512]{3,2,1,0:T(2,128)(2,1)S(1)}, u32[]{:S(2)}, u32[]{:S(2)}) collective-permute-start(bf16[2,8,1,512]{3,2,1,0:T(2,128)(2,1)S(1)} %get-tuple-element.102), channel_id=1, source_target_pairs={{2,0},{4,2},{6,4},{8,6},{10,8},{12,10},{14,12},{16,14},{18,16},{20... | collective-permute-start | bytes 49160 | tf_op jit(solution)/shard_map/ppermute | solution.py:34
  116.9 6.1 %collective-permute-start.17 = (bf16[2,8,1,512]{3,2,1,0:T(2,128)(2,1)S(1)}, bf16[2,8,1,512]{3,2,1,0:T(2,128)(2,1)S(1)}, u32[]{:S(2)}, u32[]{:S(2)}) collective-permute-start(bf16[2,8,1,512]{3,2,1,0:T(2,128)(2,1)S(1)} %get-tuple-element.101), channel_id=1, source_target_pairs={{0,2},{2,4},{4,6},{6,8},{8,10},{10,12},{12,14},{14,16},{16,18},{18... | collective-permute-start | bytes 49160 | tf_op jit(solution)/shard_map/ppermute | solution.py:32
  125.2 14.2 %collective-permute-start.31 = (bf16[2,1,16,512]{3,2,1,0:T(8,128)(2,1)S(1)}, bf16[2,1,16,512]{3,2,1,0:T(8,128)(2,1)S(1)}, u32[]{:S(2)}, u32[]{:S(2)}) collective-permute-start(bf16[2,1,16,512]{3,2,1,0:T(8,128)(2,1)S(1)} %get-tuple-element.100), channel_id=1, source_target_pairs={{1,0},{3,2},{5,4},{7,6},{9,8},{11,10},{13,12},{15,14},{17,16},{19,... | collective-permute-start | bytes 98312 | tf_op jit(solution)/shard_map/ppermute | solution.py:34
  126.5 13.1 %collective-permute-start.32 = (bf16[2,1,16,512]{3,2,1,0:T(8,128)(2,1)S(1)}, bf16[2,1,16,512]{3,2,1,0:T(8,128)(2,1)S(1)}, u32[]{:S(2)}, u32[]{:S(2)}) collective-permute-start(bf16[2,1,16,512]{3,2,1,0:T(8,128)(2,1)S(1)} %get-tuple-element.99), channel_id=1, source_target_pairs={{0,1},{2,3},{4,5},{6,7},{8,9},{10,11},{12,13},{14,15},{16,17},{18,... | collective-permute-start | bytes 98312 | tf_op jit(solution)/shard_map/ppermute | solution.py:32
  131.1 4.6 %collective-permute-start.30 = (bf16[2,8,1,512]{3,2,1,0:T(2,128)(2,1)S(1)}, bf16[2,8,1,512]{3,2,1,0:T(2,128)(2,1)S(1)}, u32[]{:S(2)}, u32[]{:S(2)}) collective-permute-start(bf16[2,8,1,512]{3,2,1,0:T(2,128)(2,1)S(1)} %get-tuple-element.96), channel_id=1, source_target_pairs={{2,0},{4,2},{6,4},{8,6},{10,8},{12,10},{14,12},{16,14},{18,16},{20... | collective-permute-start | bytes 49160 | tf_op jit(solution)/shard_map/ppermute | solution.py:34
  133.0 6.1 %collective-permute-start.29 = (bf16[2,8,1,512]{3,2,1,0:T(2,128)(2,1)S(1)}, bf16[2,8,1,512]{3,2,1,0:T(2,128)(2,1)S(1)}, u32[]{:S(2)}, u32[]{:S(2)}) collective-permute-start(bf16[2,8,1,512]{3,2,1,0:T(2,128)(2,1)S(1)} %get-tuple-element.95), channel_id=1, source_target_pairs={{0,2},{2,4},{4,6},{6,8},{8,10},{10,12},{12,14},{14,16},{16,18},{18... | collective-permute-start | bytes 49160 | tf_op jit(solution)/shard_map/ppermute | solution.py:32
  140.9 14.2 %collective-permute-start.35 = (bf16[2,1,16,512]{3,2,1,0:T(8,128)(2,1)S(1)}, bf16[2,1,16,512]{3,2,1,0:T(8,128)(2,1)S(1)}, u32[]{:S(2)}, u32[]{:S(2)}) collective-permute-start(bf16[2,1,16,512]{3,2,1,0:T(8,128)(2,1)S(1)} %get-tuple-element.94), channel_id=1, source_target_pairs={{1,0},{3,2},{5,4},{7,6},{9,8},{11,10},{13,12},{15,14},{17,16},{19,... | collective-permute-start | bytes 98312 | tf_op jit(solution)/shard_map/ppermute | solution.py:34
  142.2 13.1 %collective-permute-start.36 = (bf16[2,1,16,512]{3,2,1,0:T(8,128)(2,1)S(1)}, bf16[2,1,16,512]{3,2,1,0:T(8,128)(2,1)S(1)}, u32[]{:S(2)}, u32[]{:S(2)}) collective-permute-start(bf16[2,1,16,512]{3,2,1,0:T(8,128)(2,1)S(1)} %get-tuple-element.93), channel_id=1, source_target_pairs={{0,1},{2,3},{4,5},{6,7},{8,9},{10,11},{12,13},{14,15},{16,17},{18,... | collective-permute-start | bytes 98312 | tf_op jit(solution)/shard_map/ppermute | solution.py:32
  146.8 4.5 %collective-permute-start.34 = (bf16[2,8,1,512]{3,2,1,0:T(2,128)(2,1)S(1)}, bf16[2,8,1,512]{3,2,1,0:T(2,128)(2,1)S(1)}, u32[]{:S(2)}, u32[]{:S(2)}) collective-permute-start(bf16[2,8,1,512]{3,2,1,0:T(2,128)(2,1)S(1)} %get-tuple-element.92), channel_id=1, source_target_pairs={{2,0},{4,2},{6,4},{8,6},{10,8},{12,10},{14,12},{16,14},{18,16},{20... | collective-permute-start | bytes 49160 | tf_op jit(solution)/shard_map/ppermute | solution.py:34
  148.7 6.1 %collective-permute-start.33 = (bf16[2,8,1,512]{3,2,1,0:T(2,128)(2,1)S(1)}, bf16[2,8,1,512]{3,2,1,0:T(2,128)(2,1)S(1)}, u32[]{:S(2)}, u32[]{:S(2)}) collective-permute-start(bf16[2,8,1,512]{3,2,1,0:T(2,128)(2,1)S(1)} %get-tuple-element.91), channel_id=1, source_target_pairs={{0,2},{2,4},{4,6},{6,8},{8,10},{10,12},{12,14},{14,16},{16,18},{18... | collective-permute-start | bytes 49160 | tf_op jit(solution)/shard_map/ppermute | solution.py:32
  156.8 14.2 %collective-permute-start.39 = (bf16[2,1,16,512]{3,2,1,0:T(8,128)(2,1)S(1)}, bf16[2,1,16,512]{3,2,1,0:T(8,128)(2,1)S(1)}, u32[]{:S(2)}, u32[]{:S(2)}) collective-permute-start(bf16[2,1,16,512]{3,2,1,0:T(8,128)(2,1)S(1)} %get-tuple-element.90), channel_id=1, source_target_pairs={{1,0},{3,2},{5,4},{7,6},{9,8},{11,10},{13,12},{15,14},{17,16},{19,... | collective-permute-start | bytes 98312 | tf_op jit(solution)/shard_map/ppermute | solution.py:34
  158.1 13.1 %collective-permute-start.40 = (bf16[2,1,16,512]{3,2,1,0:T(8,128)(2,1)S(1)}, bf16[2,1,16,512]{3,2,1,0:T(8,128)(2,1)S(1)}, u32[]{:S(2)}, u32[]{:S(2)}) collective-permute-start(bf16[2,1,16,512]{3,2,1,0:T(8,128)(2,1)S(1)} %get-tuple-element.89), channel_id=1, source_target_pairs={{0,1},{2,3},{4,5},{6,7},{8,9},{10,11},{12,13},{14,15},{16,17},{18,... | collective-permute-start | bytes 98312 | tf_op jit(solution)/shard_map/ppermute | solution.py:32
  162.7 4.5 %collective-permute-start.38 = (bf16[2,8,1,512]{3,2,1,0:T(2,128)(2,1)S(1)}, bf16[2,8,1,512]{3,2,1,0:T(2,128)(2,1)S(1)}, u32[]{:S(2)}, u32[]{:S(2)}) collective-permute-start(bf16[2,8,1,512]{3,2,1,0:T(2,128)(2,1)S(1)} %get-tuple-element.88), channel_id=1, source_target_pairs={{2,0},{4,2},{6,4},{8,6},{10,8},{12,10},{14,12},{16,14},{18,16},{20... | collective-permute-start | bytes 49160 | tf_op jit(solution)/shard_map/ppermute | solution.py:34
  164.6 6.1 %collective-permute-start.37 = (bf16[2,8,1,512]{3,2,1,0:T(2,128)(2,1)S(1)}, bf16[2,8,1,512]{3,2,1,0:T(2,128)(2,1)S(1)}, u32[]{:S(2)}, u32[]{:S(2)}) collective-permute-start(bf16[2,8,1,512]{3,2,1,0:T(2,128)(2,1)S(1)} %get-tuple-element.87), channel_id=1, source_target_pairs={{0,2},{2,4},{4,6},{6,8},{8,10},{10,12},{12,14},{14,16},{16,18},{18... | collective-permute-start | bytes 49160 | tf_op jit(solution)/shard_map/ppermute | solution.py:32
where the time goes:
time: 174 us; the launch traced here: 173 us
  waiting for transfers between devices  78.6 us (45%)
  starting transfers between devices  75.4 us (43%)
  other arithmetic  17.1 us (10%)
    ppermute x17, waiting for transfers between devices, from_behind(): lax.ppermute(value, axis, [(i, (i + by) % peers) for i in range(peers)])  57.4 us
    ppermute x12, starting transfers between devices, padded_2(): lax.ppermute(tail, axis, [(i, (i + 1) % count) for i in range(ends)])  40.9 us
    ppermute x12, starting transfers between devices, padded_2(): lax.ppermute(head, axis, [((i + 1) % count, i) for i in range(ends)])  25.7 us
    ppermute x12, waiting for transfers between devices, padded_2(): lax.ppermute(tail, axis, [(i, (i + 1) % count) for i in range(ends)])  21.1 us
    ppermute x17, starting transfers between devices, from_behind(): lax.ppermute(value, axis, [(i, (i + by) % peers) for i in range(peers)])  8.75 us
    mul x6, other arithmetic, along_range(): return 0.5 * (padded[..., 2:] - padded[..., :-2])  5.92 us
  transfers between devices with their start and end apart: 41, of which 21 were waited for; matrix products, arithmetic and copies ran while one was open for 4% of the time, Pallas kernels for 0%

commit v1 on v0

v1 whole, which is shorter than its diff:
```python
import functools
import math

import jax
import jax.numpy as jnp
from jax import lax
from jax.experimental import pallas as pl
from jax.experimental.pallas import tpu as pltpu
from jax.sharding import PartitionSpec as P

section_keep = (0.0, -5.0 / 9.0, -153.0 / 128.0)
section_gain = (1.0 / 3.0, 15.0 / 16.0, 8.0 / 15.0)
time_step = 0.4
half_step = 0.5 * time_step
MESH = pl.DeviceIdType.MESH


def kernel(
    n, floors, steps, levels, rows, cols, width,
    state_ref, turb_ref, wind_ref, adm_ref, kind_ref, cells_ref, eighths_ref,
    out_ref,
    pa, ua, va, wa, pb, ub, vb, wb, chg, adv, sqr, gath, outb, froz,
    rsend, rrecv, hsend, hrecv,
    in_sem, s1, r1, s2, r2, rs, rr, hs, hr,
):
    me = lax.axis_index("cross")
    floor = lax.axis_index("height")
    length = n * rows
    pieces = cols // width
    sections = 3 * steps

    def part(j):
        field = j // (levels * pieces)
        rest = j % (levels * pieces)
        return field, rest // pieces, pl.multiple_of((rest % pieces) * width, width)

    def peer(k):
        return lax.rem(me + k, n)

    def rows_of(j):
        return pl.ds(pl.multiple_of(j * rows, rows), rows)

    has_left, has_right = me > 0, me < n - 1
    has_below, has_above = floor > 0, floor < floors - 1

    loads = [
        pltpu.make_async_copy(state_ref.at[0], pa.at[pl.ds(1, levels)], in_sem.at[0]),
        pltpu.make_async_copy(state_ref.at[1], ua, in_sem.at[1]),
        pltpu.make_async_copy(state_ref.at[2], va, in_sem.at[2]),
        pltpu.make_async_copy(state_ref.at[3], wa.at[pl.ds(1, levels)], in_sem.at[3]),
    ]
    for load in loads:
        load.start()

    barrier = pltpu.get_barrier_semaphore()

    def greet(k, carry):
        pl.semaphore_signal(barrier, inc=1, device_id={"cross": peer(k)}, device_id_type=MESH)
        return carry

    lax.fori_loop(1, n, greet, 0)

    @pl.when(has_below)
    def _():
        pl.semaphore_signal(barrier, inc=1, device_id={"height": floor - 1}, device_id_type=MESH)

    @pl.when(has_above)
    def _():
        pl.semaphore_signal(barrier, inc=1, device_id={"height": floor + 1}, device_id_type=MESH)

    zero_rows = jnp.zeros((2 * levels, cols), jnp.float32)
    for k in range(sections):
        @pl.when(jnp.logical_not(has_left))
        def _():
            rrecv[k, 0] = zero_rows

        @pl.when(jnp.logical_not(has_right))
        def _():
            rrecv[k, 1] = zero_rows

    pl.semaphore_wait(
        barrier, n - 1 + has_below.astype(jnp.int32) + has_above.astype(jnp.int32)
    )

    def gather_copy(k):
        to = peer(k)
        field, level, at = part(to)
        return pltpu.make_async_remote_copy(
            src_ref=turb_ref.at[field, level, :, pl.ds(at, width)],
            dst_ref=gath.at[rows_of(me)],
            send_sem=s1.at[to],
            recv_sem=r1.at[me],
            device_id={"cross": to},
            device_id_type=MESH,
        )

    def gather_wait(k):
        source = peer(k)
        return pltpu.make_async_remote_copy(
            src_ref=gath.at[rows_of(source)],
            dst_ref=gath.at[rows_of(source)],
            send_sem=s1.at[source],
            recv_sem=r1.at[source],
            device_id={"cross": source},
            device_id_type=MESH,
        )

    def start_gather(k, carry):
        gather_copy(k).start()
        return carry

    lax.fori_loop(1, n, start_gather, 0)
    my_field, my_level, my_at = part(me)
    own = pltpu.make_async_copy(
        turb_ref.at[my_field, my_level, :, pl.ds(my_at, width)], gath.at[rows_of(me)], in_sem.at[4]
    )
    own.start()

    def row_copy(k, side):
        to = me - 1 if side == 0 else me + 1
        return pltpu.make_async_remote_copy(
            src_ref=rsend.at[k, side],
            dst_ref=rrecv.at[k, 1 - side],
            send_sem=rs.at[k, side],
            recv_sem=rr.at[k, 1 - side],
            device_id={"cross": to},
            device_id_type=MESH,
        )

    def level_copy(k, side):
        to = floor - 1 if side == 0 else floor + 1
        return pltpu.make_async_remote_copy(
            src_ref=hsend.at[k, side],
            dst_ref=hrecv.at[k, 1 - side],
            send_sem=hs.at[k, side],
            recv_sem=hr.at[k, 1 - side],
            device_id={"height": to},
            device_id_type=MESH,
        )

    def send_rows(k):
        @pl.when(has_left)
        def _():
            row_copy(k, 0).start()

        @pl.when(has_right)
        def _():
            row_copy(k, 1).start()

    def send_levels(k, pn, wn):
        @pl.when(has_below)
        def _():
            hsend[k, 0, 0] = pn[1].astype(jnp.bfloat16)
            hsend[k, 0, 1] = wn[1].astype(jnp.bfloat16)
            level_copy(k, 0).start()

        @pl.when(has_above)
        def _():
            hsend[k, 1, 0] = pn[levels].astype(jnp.bfloat16)
            hsend[k, 1, 1] = wn[levels].astype(jnp.bfloat16)
            level_copy(k, 1).start()

    def receive(k, pn, wn):
        @pl.when(has_below)
        def _():
            level_copy(k, 1).wait_recv()
            pn[0] = hrecv[k, 0, 0].astype(jnp.float32)
            wn[0] = hrecv[k, 0, 1].astype(jnp.float32)

        @pl.when(jnp.logical_not(has_below))
        def _():
            ground = 2.0 * adm_ref[...] * kind_ref[...].astype(jnp.float32)
            low = pn[1]
            pn[0] = low
            wn[0] = ground * low - wn[1]

        @pl.when(has_above)
        def _():
            level_copy(k, 0).wait_recv()
            pn[levels + 1] = hrecv[k, 1, 0].astype(jnp.float32)
            wn[levels + 1] = hrecv[k, 1, 1].astype(jnp.float32)

        @pl.when(jnp.logical_not(has_above))
        def _():
            pn[levels + 1] = jnp.zeros((rows, cols), jnp.float32)
            wn[levels + 1] = jnp.zeros((rows, cols), jnp.float32)

        @pl.when(has_left)
        def _():
            row_copy(k, 1).wait_recv()

        @pl.when(has_right)
        def _():
            row_copy(k, 0).wait_recv()

    for load in loads:
        load.wait()

    def first_rows(level, carry):
        for field, ref, offset in ((0, pa, 1), (1, va, 0)):
            rsend[0, 0, pl.ds(field * levels + level, 1)] = ref[level + offset, pl.ds(0, 1)]
            rsend[0, 1, pl.ds(field * levels + level, 1)] = ref[level + offset, pl.ds(rows - 1, 1)]
        return carry

    lax.fori_loop(0, levels, first_rows, 0)
    send_rows(0)
    send_levels(0, pa, wa)

    own.wait()

    def whole(k, carry):
        gather_wait(k).wait_recv()
        return carry

    lax.fori_loop(1, n, whole, 0)
    block = math.gcd(length, 256)

    def spread_copy(step, k):
        to = peer(k)
        return pltpu.make_async_remote_copy(
            src_ref=outb.at[step, rows_of(to)],
            dst_ref=froz.at[step, my_field, my_level, :, pl.ds(my_at, width)],
            send_sem=s2.at[step, to],
            recv_sem=r2.at[step, me],
            device_id={"cross": to},
            device_id_type=MESH,
        )

    def spread_wait(step, k):
        source = peer(k)
        field, level, at = part(source)
        return pltpu.make_async_remote_copy(
            src_ref=outb.at[step, rows_of(source)],
            dst_ref=froz.at[step, field, level, :, pl.ds(at, width)],
            send_sem=s2.at[step, source],
            recv_sem=r2.at[step, source],
            device_id={"cross": source},
            device_id_type=MESH,
        )

    for step in range(steps):
        cells = cells_ref[step, my_level]
        weight = eighths_ref[step, my_level].astype(jnp.float32) / 8.0

        def mix(i, carry, step=step, cells=cells, weight=weight):
            top = pl.multiple_of(i * block, block)
            to_row = lax.broadcasted_iota(jnp.int32, (block, length), 0) + top
            from_row = lax.broadcasted_iota(jnp.int32, (block, length), 1)
            back = to_row - from_row - cells
            back = jnp.where(back < 0, back + length, back)
            back = jnp.where(back < 0, back + length, back)
            share = jnp.where(back == 0, 1.0 - weight, jnp.where(back == 1, weight, 0.0))
            outb[step, pl.ds(top, block)] = jnp.dot(
                share.astype(jnp.bfloat16), gath[...], preferred_element_type=jnp.float32
            ).astype(jnp.bfloat16)
            return carry

        lax.fori_loop(0, length // block, mix, 0)

        def spread(k, carry, step=step):
            spread_copy(step, k).start()
            return carry

        lax.fori_loop(1, n, spread, 0)
        froz[step, my_field, my_level, :, pl.ds(my_at, width)] = outb[step, rows_of(me)]

    row_id = lax.broadcasted_iota(jnp.int32, (rows, cols), 0)
    col_id = lax.broadcasted_iota(jnp.int32, (rows, cols), 1)

    def d_range(f):
        ahead = jnp.where(col_id == cols - 1, 0.0, pltpu.roll(f, cols - 1, 1))
        behind = jnp.where(col_id == 0, 0.0, pltpu.roll(f, 1, 1))
        return ahead - behind

    def d_cross(f, before, after):
        ahead = jnp.where(row_id == rows - 1, after, pltpu.roll(f, rows - 1, 0))
        behind = jnp.where(row_id == 0, before, pltpu.roll(f, 1, 0))
        return ahead - behind

    sets = ((pa, ua, va, wa), (pb, ub, vb, wb))
    for k in range(sections):
        step, section = k // 3, k % 3
        po, uo, vo, wo = sets[k % 2]
        pn, un, vn, wn = sets[(k + 1) % 2]
        last = k == sections - 1
        if section == 0:
            def arrive(j, carry, step=step):
                spread_wait(step, j).wait_recv()
                return carry

            lax.fori_loop(1, n, arrive, 0)
        receive(k, po, wo)
        keep, gain = section_keep[section], section_gain[section]

        def update(level, carry):
            if section == 0:
                frozen = froz[step, 0, level].astype(jnp.float32)
                speed = 1.0 + froz[step, 1, level].astype(jnp.float32)
                advect = half_step * (wind_ref[level] + frozen)
                squared = half_step * (speed * speed)
                adv[level] = advect
                sqr[level] = squared
            else:
                advect = adv[level]
                squared = sqr[level]
            p, u, v, w = po[level + 1], uo[level], vo[level], wo[level + 1]
            p_x, u_x, v_x, w_x = d_range(p), d_range(u), d_range(v), d_range(w)
            p_y = d_cross(p, rrecv[k, 0, pl.ds(level, 1)], rrecv[k, 1, pl.ds(level, 1)])
            v_y = d_cross(
                v, rrecv[k, 0, pl.ds(levels + level, 1)], rrecv[k, 1, pl.ds(levels + level, 1)]
            )
            p_z = po[level + 2] - po[level]
            w_z = wo[level + 2] - wo[level]
            fresh = (
                advect * p_x + squared * (u_x + v_y + w_z),
                advect * u_x + half_step * p_x,
                advect * v_x + half_step * p_y,
                advect * w_x + half_step * p_z,
            )
            new = []
            for field, (rate, old) in enumerate(zip(fresh, (p, u, v, w))):
                change = -rate if section == 0 else keep * chg[field, level] - rate
                if section < 2:
                    chg[field, level] = change
                new.append(old + gain * change)
            if last:
                for field in range(4):
                    out_ref[field, level] = new[field]
            else:
                pn[level + 1], un[level], vn[level], wn[level + 1] = new
                for field, value in ((0, new[0]), (1, new[2])):
                    rsend[k + 1, 0, pl.ds(field * levels + level, 1)] = value[0:1]
                    rsend[k + 1, 1, pl.ds(field * levels + level, 1)] = value[rows - 1 : rows]
            return carry

        lax.fori_loop(0, levels, update, 0)
        if not last:
            send_rows(k + 1)
            send_levels(k + 1, pn, wn)

    def left(k, carry):
        gather_copy(k).wait_send()
        for step in range(steps):
            spread_copy(step, k).wait_send()
        return carry

    lax.fori_loop(1, n, left, 0)
    for k in range(sections):
        for side, there in ((0, has_left), (1, has_right)):
            @pl.when(there)
            def _():
                row_copy(k, side).wait_send()
        for side, there in ((0, has_below), (1, has_above)):
            @pl.when(there)
            def _():
                level_copy(k, side).wait_send()


def body(n, floors, state, turbulence, wind, ground_admittance, ground_kind, drift_cells, drift_eighths):
    fields, levels, rows, cols = state.shape
    steps = drift_cells.shape[0]
    sections = 3 * steps
    width = 2 * levels * cols // n
    f32, bf16 = jnp.float32, jnp.bfloat16
    padded = pltpu.VMEM((levels + 2, rows, cols), f32)
    plain = pltpu.VMEM((levels, rows, cols), f32)
    dma = pltpu.SemaphoreType.DMA
    vmem = pl.BlockSpec(memory_space=pltpu.VMEM)
    smem = pl.BlockSpec(memory_space=pltpu.SMEM)
    hbm = pl.BlockSpec(memory_space=pl.ANY)
    return pl.pallas_call(
        functools.partial(kernel, n, floors, steps, levels, rows, cols, width),
        out_shape=jax.ShapeDtypeStruct(state.shape, f32),
        in_specs=[hbm, vmem, smem, vmem, vmem, smem, smem],
        out_specs=vmem,
        scratch_shapes=[
            padded, plain, plain, padded,
            padded, plain, plain, padded,
            pltpu.VMEM((fields, levels, rows, cols), f32),
            plain,
            plain,
            pltpu.VMEM((n * rows, width), bf16),
            pltpu.VMEM((steps, n * rows, width), bf16),
            pltpu.VMEM((steps, 2, levels, rows, cols), bf16),
            pltpu.VMEM((sections, 2, 2 * levels, cols), f32),
            pltpu.VMEM((sections, 2, 2 * levels, cols), f32),
            pltpu.VMEM((sections, 2, 2, rows, cols), bf16),
            pltpu.VMEM((sections, 2, 2, rows, cols), bf16),
            dma((5,)),
            dma((n,)), dma((n,)),
            dma((steps, n)), dma((steps, n)),
            dma((sections, 2)), dma((sections, 2)),
            dma((sections, 2)), dma((sections, 2)),
        ],
        compiler_params=pltpu.CompilerParams(
            collective_id=0, has_side_effects=True, vmem_limit_bytes=40 * 2**20
        ),
    )(state, turbulence, wind, ground_admittance, ground_kind, drift_cells, drift_eighths)


def solution(mesh):
    placed = (
        P(None, "height", "cross", None),
        P(None, "height", "cross", None),
        P("height"),
        P("cross", None),
        P("cross", None),
        P(None, "height"),
        P(None, "height"),
    )
    return jax.shard_map(
        functools.partial(body, mesh.shape["cross"], mesh.shape["height"]),
        mesh=mesh,
        in_specs=placed,
        out_specs=P(None, "height", "cross", None),
        check_vma=False,
    )
```

time: 174 us -> 52.5 us (0.30)
  the two profiles are of different devices: /device:TPU:8 before, /device:TPU:13 now
where the time goes in v1:
time: 52.5 us; the launch traced here: 52.1 us
  Pallas kernels  45.5 us (87%)
  local copies, waits for them, and re-layouts  6.67 us (13%)
    pallas_call x1, Pallas kernels, body(): pl.pallas_call(functools.partial(kernel, n, floors, steps, levels, rows,...  45.5 us
    unnamed x15, local copies, waits for them, and re-layouts  6.67 us

profile of v1, /device:TPU:13, one launch (start us, length us, event | category | flops | bytes accessed | tf_op | source)
XLA Modules:
  0.0 52.1 jit_solution(17721437159178919304)
XLA Ops:
  0.0 0.0 copy-start
  0.0 1.2 %copy-done = f32[4,8,16,512]{3,2,1,0:T(8,128)S(1)} copy-done((f32[4,8,16,512]{3,2,1,0:T(8,128)S(1)}, f32[4,8,16,512]{3,2,1,0:T(8,128)}, u32[]{:S(2)}) %copy-start) | copy-done | bytes 1048600
  1.2 0.0 copy-start.1
  1.2 0.9 %copy-done.1 = bf16[2,8,16,512]{3,2,1,0:T(8,128)(2,1)S(1)} copy-done((bf16[2,8,16,512]{3,2,1,0:T(8,128)(2,1)S(1)}, bf16[2,8,16,512]{3,2,1,0:T(8,128)(2,1)}, u32[]{:S(2)}) %copy-start.1) | copy-done | bytes 262168
  2.2 0.0 copy-start.2
  2.2 0.8 %copy-done.2 = f32[16,512]{1,0:T(8,128)S(1)} copy-done((f32[16,512]{1,0:T(8,128)S(1)}, f32[16,512]{1,0:T(8,128)}, u32[]{:S(2)}) %copy-start.2) | copy-done | bytes 32792
  2.9 0.0 copy-start.3
  2.9 0.8 %copy-done.3 = s32[16,512]{1,0:T(8,128)S(1)} copy-done((s32[16,512]{1,0:T(8,128)S(1)}, s32[16,512]{1,0:T(8,128)}, u32[]{:S(2)}) %copy-start.3) | copy-done | bytes 32792
  3.7 0.0 copy-start.4
  3.7 0.7 %copy-done.4 = s32[2,8]{1,0:T(2,128)S(1)} copy-done((s32[2,8]{1,0:T(2,128)S(1)}, s32[2,8]{1,0:T(2,128)}, u32[]{:S(2)}) %copy-start.4) | copy-done | bytes 88
  4.4 0.0 copy-start.5
  4.4 0.7 %copy-done.5 = s32[2,8]{1,0:T(2,128)S(1)} copy-done((s32[2,8]{1,0:T(2,128)S(1)}, s32[2,8]{1,0:T(2,128)}, u32[]{:S(2)}) %copy-start.5) | copy-done | bytes 88
  5.1 0.0 copy-start.6
  5.1 0.7 %copy-done.6 = f32[8]{0:T(128)S(1)} copy-done((f32[8]{0:T(128)S(1)}, f32[8]{0:T(128)}, u32[]{:S(2)}) %copy-start.6) | copy-done | bytes 56
  5.7 45.5 %shard_map.73 = f32[4,8,16,512]{3,2,1,0:T(8,128)S(1)} custom-call(f32[4,8,16,512]{3,2,1,0:T(8,128)S(1)} %copy-done, bf16[2,8,16,512]{3,2,1,0:T(8,128)(2,1)S(1)} %copy-done.1, f32[8]{0:T(128)S(1)} %copy-done.6, f32[16,512]{1,0:T(8,128)S(1)} %copy-done.2, s32[16,512]{1,0:T(8,128)S(1)} %copy-done.3, s32[2,8]{1,0:T(2,128)S(1)} %copy-done.4, s32[2,8]{1,0:T(2,128)S(1)} %copy-done.5), custom_call_target="tpu_custom_call" | custom-call | tf_op jit(solution)/shard_map/pallas_call | solution.py:371
  51.2 1.0 %copy.9 = f32[4,8,16,512]{3,2,1,0:T(8,128)} copy(f32[4,8,16,512]{3,2,1,0:T(8,128)S(1)} %shard_map.73) | data formatting | bytes 2097152
Async XLA Ops:
  0.0 1.2 %copy-start = (f32[4,8,16,512]{3,2,1,0:T(8,128)S(1)}, f32[4,8,16,512]{3,2,1,0:T(8,128)}, u32[]{:S(2)}) copy-start(f32[4,8,16,512]{3,2,1,0:T(8,128)} %state_ref.1) | copy-start | bytes 3145732
  1.2 0.9 %copy-start.1 = (bf16[2,8,16,512]{3,2,1,0:T(8,128)(2,1)S(1)}, bf16[2,8,16,512]{3,2,1,0:T(8,128)(2,1)}, u32[]{:S(2)}) copy-start(bf16[2,8,16,512]{3,2,1,0:T(8,128)(2,1)} %turb_ref.1) | copy-start | bytes 786436
  2.2 0.8 %copy-start.2 = (f32[16,512]{1,0:T(8,128)S(1)}, f32[16,512]{1,0:T(8,128)}, u32[]{:S(2)}) copy-start(f32[16,512]{1,0:T(8,128)} %adm_ref.1) | copy-start | bytes 98308
  2.9 0.8 %copy-start.3 = (s32[16,512]{1,0:T(8,128)S(1)}, s32[16,512]{1,0:T(8,128)}, u32[]{:S(2)}) copy-start(s32[16,512]{1,0:T(8,128)} %kind_ref.1) | copy-start | bytes 98308
  3.7 0.7 %copy-start.4 = (s32[2,8]{1,0:T(2,128)S(1)}, s32[2,8]{1,0:T(2,128)}, u32[]{:S(2)}) copy-start(s32[2,8]{1,0:T(2,128)} %cells_ref.1) | copy-start | bytes 196
  4.4 0.7 %copy-start.5 = (s32[2,8]{1,0:T(2,128)S(1)}, s32[2,8]{1,0:T(2,128)}, u32[]{:S(2)}) copy-start(s32[2,8]{1,0:T(2,128)} %eighths_ref.1) | copy-start | bytes 196
  5.1 0.7 %copy-start.6 = (f32[8]{0:T(128)S(1)}, f32[8]{0:T(128)}, u32[]{:S(2)}) copy-start(f32[8]{0:T(128)} %wind_ref.1) | copy-start | bytes 100

commit v2 on v1

--- a/solution.py
+++ b/solution.py
@@ -17,17 +17,19 @@
 
 def kernel(
     n, floors, steps, levels, rows, cols, width,
-    state_ref, turb_ref, wind_ref, adm_ref, kind_ref, cells_ref, eighths_ref,
+    state_ref, turb_ref, wind_in, adm_in, kind_in, cells_in, eighths_in,
     out_ref,
+    wind_ref, adm_ref, kind_ref, cells_ref, eighths_ref,
     pa, ua, va, wa, pb, ub, vb, wb, chg, adv, sqr, gath, outb, froz,
     rsend, rrecv, hsend, hrecv,
-    in_sem, s1, r1, s2, r2, rs, rr, hs, hr,
+    in_sem, out_sem, s1, r1, s2, r2, rs, rr, hs, hr,
 ):
     me = lax.axis_index("cross")
     floor = lax.axis_index("height")
     length = n * rows
     pieces = cols // width
     sections = 3 * steps
+    half = levels // 2
 
     def part(j):
         field = j // (levels * pieces)
@@ -48,6 +50,11 @@
         pltpu.make_async_copy(state_ref.at[1], ua, in_sem.at[1]),
         pltpu.make_async_copy(state_ref.at[2], va, in_sem.at[2]),
         pltpu.make_async_copy(state_ref.at[3], wa.at[pl.ds(1, levels)], in_sem.at[3]),
+        pltpu.make_async_copy(wind_in, wind_ref, in_sem.at[5]),
+        pltpu.make_async_copy(adm_in, adm_ref, in_sem.at[6]),
+        pltpu.make_async_copy(kind_in, kind_ref, in_sem.at[7]),
+        pltpu.make_async_copy(cells_in, cells_ref, in_sem.at[8]),
+        pltpu.make_async_copy(eighths_in, eighths_ref, in_sem.at[9]),
     ]
     for load in loads:
         load.start()
@@ -116,13 +123,14 @@
     )
     own.start()
 
-    def row_copy(k, side):
+    def row_copy(k, side, group):
         to = me - 1 if side == 0 else me + 1
-        return pltpu.make_async_remote_copy(
-            src_ref=rsend.at[k, side],
-            dst_ref=rrecv.at[k, 1 - side],
-            send_sem=rs.at[k, side],
-            recv_sem=rr.at[k, 1 - side],
+        lines = pl.ds(2 * half * group, 2 * half)
+        return pltpu.make_async_remote_copy(
+            src_ref=rsend.at[k, side, lines],
+            dst_ref=rrecv.at[k, 1 - side, lines],
+            send_sem=rs.at[k, side, group],
+            recv_sem=rr.at[k, 1 - side, group],
             device_id={"cross": to},
             device_id_type=MESH,
         )
@@ -138,29 +146,39 @@
             device_id_type=MESH,
         )
 
-    def send_rows(k):
+    def send_rows(k, group):
         @pl.when(has_left)
         def _():
-            row_copy(k, 0).start()
+            row_copy(k, 0, group).start()
 
         @pl.when(has_right)
         def _():
-            row_copy(k, 1).start()
-
-    def send_levels(k, pn, wn):
+            row_copy(k, 1, group).start()
+
+    def receive_rows(k, group):
+        @pl.when(has_left)
+        def _():
+            row_copy(k, 1, group).wait_recv()
+
+        @pl.when(has_right)
+        def _():
+            row_copy(k, 0, group).wait_recv()
+
+    def send_down(k, pn, wn):
         @pl.when(has_below)
         def _():
             hsend[k, 0, 0] = pn[1].astype(jnp.bfloat16)
             hsend[k, 0, 1] = wn[1].astype(jnp.bfloat16)
             level_copy(k, 0).start()
 
+    def send_up(k, pn, wn):
         @pl.when(has_above)
         def _():
             hsend[k, 1, 0] = pn[levels].astype(jnp.bfloat16)
             hsend[k, 1, 1] = wn[levels].astype(jnp.bfloat16)
             level_copy(k, 1).start()
 
-    def receive(k, pn, wn):
+    def receive_below(k, pn, wn):
         @pl.when(has_below)
         def _():
             level_copy(k, 1).wait_recv()
@@ -174,6 +192,7 @@
             pn[0] = low
             wn[0] = ground * low - wn[1]
 
+    def receive_above(k, pn, wn):
         @pl.when(has_above)
         def _():
             level_copy(k, 0).wait_recv()
@@ -185,26 +204,20 @@
             pn[levels + 1] = jnp.zeros((rows, cols), jnp.float32)
             wn[levels + 1] = jnp.zeros((rows, cols), jnp.float32)
 
-        @pl.when(has_left)
-        def _():
-            row_copy(k, 1).wait_recv()
-
-        @pl.when(has_right)
-        def _():
-            row_copy(k, 0).wait_recv()
-
     for load in loads:
         load.wait()
 
     def first_rows(level, carry):
         for field, ref, offset in ((0, pa, 1), (1, va, 0)):
-            rsend[0, 0, pl.ds(field * levels + level, 1)] = ref[level + offset, pl.ds(0, 1)]
-            rsend[0, 1, pl.ds(field * levels + level, 1)] = ref[level + offset, pl.ds(rows - 1, 1)]
+            rsend[0, 0, pl.ds(2 * level + field, 1)] = ref[level + offset, pl.ds(0, 1)]
+            rsend[0, 1, pl.ds(2 * level + field, 1)] = ref[level + offset, pl.ds(rows - 1, 1)]
         return carry
 
     lax.fori_loop(0, levels, first_rows, 0)
-    send_rows(0)
-    send_levels(0, pa, wa)
+    send_down(0, pa, wa)
+    send_rows(0, 0)
+    send_up(0, pa, wa)
+    send_rows(0, 1)
 
     own.wait()
 
@@ -237,6 +250,13 @@
             device_id={"cross": source},
             device_id_type=MESH,
         )
+
+    def spread_some(step, third, of):
+        def spread(k, carry):
+            spread_copy(step, k).start()
+            return carry
+
+        lax.fori_loop(1 + (n - 1) * third // of, 1 + (n - 1) * (third + 1) // of, spread, 0)
 
     for step in range(steps):
         cells = cells_ref[step, my_level]
@@ -257,11 +277,8 @@
 
         lax.fori_loop(0, length // block, mix, 0)
 
-        def spread(k, carry, step=step):
-            spread_copy(step, k).start()
-            return carry
-
-        lax.fori_loop(1, n, spread, 0)
+        if step == 0:
+            spread_some(0, 0, 1)
         froz[step, my_field, my_level, :, pl.ds(my_at, width)] = outb[step, rows_of(me)]
 
     row_id = lax.broadcasted_iota(jnp.int32, (rows, cols), 0)
@@ -276,6 +293,9 @@
         ahead = jnp.where(row_id == rows - 1, after, pltpu.roll(f, rows - 1, 0))
         behind = jnp.where(row_id == 0, before, pltpu.roll(f, 1, 0))
         return ahead - behind
+
+    def out_copy(level):
+        return pltpu.make_async_copy(chg.at[:, level], out_ref.at[:, level], out_sem.at[level])
 
     sets = ((pa, ua, va, wa), (pb, ub, vb, wb))
     for k in range(sections):
@@ -289,10 +309,20 @@
                 return carry
 
             lax.fori_loop(1, n, arrive, 0)
-        receive(k, po, wo)
+        if step + 1 < steps:
+            spread_some(step + 1, section, 3)
+        receive_below(k, po, wo)
+        receive_rows(k, 0)
         keep, gain = section_keep[section], section_gain[section]
 
-        def update(level, carry):
+        def update(i, carry):
+            level = jnp.where(i < half, i, jnp.where(i == half, levels - 1, i - 1))
+
+            @pl.when(i == half)
+            def _():
+                receive_above(k, po, wo)
+                receive_rows(k, 1)
+
             if section == 0:
                 frozen = froz[step, 0, level].astype(jnp.float32)
                 speed = 1.0 + froz[step, 1, level].astype(jnp.float32)
@@ -305,9 +335,9 @@
                 squared = sqr[level]
             p, u, v, w = po[level + 1], uo[level], vo[level], wo[level + 1]
             p_x, u_x, v_x, w_x = d_range(p), d_range(u), d_range(v), d_range(w)
-            p_y = d_cross(p, rrecv[k, 0, pl.ds(level, 1)], rrecv[k, 1, pl.ds(level, 1)])
+            p_y = d_cross(p, rrecv[k, 0, pl.ds(2 * level, 1)], rrecv[k, 1, pl.ds(2 * level, 1)])
             v_y = d_cross(
-                v, rrecv[k, 0, pl.ds(levels + level, 1)], rrecv[k, 1, pl.ds(levels + level, 1)]
+                v, rrecv[k, 0, pl.ds(2 * level + 1, 1)], rrecv[k, 1, pl.ds(2 * level + 1, 1)]
             )
             p_z = po[level + 2] - po[level]
             w_z = wo[level + 2] - wo[level]
@@ -325,18 +355,37 @@
                 new.append(old + gain * change)
             if last:
                 for field in range(4):
-                    out_ref[field, level] = new[field]
+                    chg[field, level] = new[field]
+                out_copy(level).start()
             else:
                 pn[level + 1], un[level], vn[level], wn[level + 1] = new
                 for field, value in ((0, new[0]), (1, new[2])):
-                    rsend[k + 1, 0, pl.ds(field * levels + level, 1)] = value[0:1]
-                    rsend[k + 1, 1, pl.ds(field * levels + level, 1)] = value[rows - 1 : rows]
+                    rsend[k + 1, 0, pl.ds(2 * level + field, 1)] = value[0:1]
+                    rsend[k + 1, 1, pl.ds(2 * level + field, 1)] = value[rows - 1 : rows]
+
+                @pl.when(i == 0)
+                def _():
+                    send_down(k + 1, pn, wn)
+
+                @pl.when(i == half - 1)
+                def _():
+                    send_rows(k + 1, 0)
+
+                @pl.when(i == half)
+                def _():
+                    send_up(k + 1, pn, wn)
+
             return carry
 
         lax.fori_loop(0, levels, update, 0)
         if not last:
-            send_rows(k + 1)
-            send_levels(k + 1, pn, wn)
+            send_rows(k + 1, 1)
+
+    def stored(level, carry):
+        out_copy(level).wait()
+        return carry
+
+    lax.fori_loop(0, levels, stored, 0)
 
     def left(k, carry):
         gather_copy(k).wait_send()
@@ -349,7 +398,8 @@
         for side, there in ((0, has_left), (1, has_right)):
             @pl.when(there)
             def _():
-                row_copy(k, side).wait_send()
+                row_copy(k, side, 0).wait_send()
+                row_copy(k, side, 1).wait_send()
         for side, there in ((0, has_below), (1, has_above)):
             @pl.when(there)
             def _():
@@ -365,15 +415,18 @@
     padded = pltpu.VMEM((levels + 2, rows, cols), f32)
     plain = pltpu.VMEM((levels, rows, cols), f32)
     dma = pltpu.SemaphoreType.DMA
-    vmem = pl.BlockSpec(memory_space=pltpu.VMEM)
-    smem = pl.BlockSpec(memory_space=pltpu.SMEM)
     hbm = pl.BlockSpec(memory_space=pl.ANY)
     return pl.pallas_call(
         functools.partial(kernel, n, floors, steps, levels, rows, cols, width),
         out_shape=jax.ShapeDtypeStruct(state.shape, f32),
-        in_specs=[hbm, vmem, smem, vmem, vmem, smem, smem],
-        out_specs=vmem,
+        in_specs=[hbm] * 7,
+        out_specs=hbm,
         scratch_shapes=[
+            pltpu.SMEM((levels,), f32),
+            pltpu.VMEM((rows, cols), f32),
+            pltpu.VMEM((rows, cols), jnp.int32),
+            pltpu.SMEM((steps, levels), jnp.int32),
+            pltpu.SMEM((steps, levels), jnp.int32),
             padded, plain, plain, padded,
             padded, plain, plain, padded,
             pltpu.VMEM((fields, levels, rows, cols), f32),
@@ -386,14 +439,14 @@
             pltpu.VMEM((sections, 2, 2 * levels, cols), f32),
             pltpu.VMEM((sections, 2, 2, rows, cols), bf16),
             pltpu.VMEM((sections, 2, 2, rows, cols), bf16),
-            dma((5,)),
+            dma((10,)), dma((levels,)),
             dma((n,)), dma((n,)),
             dma((steps, n)), dma((steps, n)),
-            dma((sections, 2)), dma((sections, 2)),
+            dma((sections, 2, 2)), dma((sections, 2, 2)),
             dma((sections, 2)), dma((sections, 2)),
         ],
         compiler_params=pltpu.CompilerParams(
-            collective_id=0, has_side_effects=True, vmem_limit_bytes=40 * 2**20
+            collective_id=0, has_side_effects=True, vmem_limit_bytes=60 * 2**20
         ),
     )(state, turbulence, wind, ground_admittance, ground_kind, drift_cells, drift_eighths)
 

time: 52.5 us -> 43.8 us (0.83)
  Pallas kernels: 45.5 us -> 40.9 us
  local copies, waits for them, and re-layouts: 6.67 us -> 2.31 us
    pallas_call x1, Pallas kernels: 45.5 us -> 40.9 us  [body(): pl.pallas_call(functools.partial(kernel, n, floors, steps, levels, rows,...]
    unnamed x15 -> x1, local copies, waits for them, and re-layouts: 6.67 us -> 2.31 us
where the time goes in v2:
time: 43.8 us; the launch traced here: 43.3 us
  Pallas kernels  40.9 us (93%)
  local copies, waits for them, and re-layouts  2.31 us (5%)
    pallas_call x1, Pallas kernels, body(): pl.pallas_call(functools.partial(kernel, n, floors, steps, levels, rows,...  40.9 us
    unnamed x1, local copies, waits for them, and re-layouts  2.31 us

profile of v2, /device:TPU:13, one launch (start us, length us, event | category | flops | bytes accessed | tf_op | source)
XLA Modules:
  0.0 43.3 jit_solution(8453497712794138788)
XLA Ops:
  0.0 40.9 %shard_map.73 = f32[4,8,16,512]{3,2,1,0:T(8,128)} custom-call(f32[4,8,16,512]{3,2,1,0:T(8,128)} %state_ref.1, bf16[2,8,16,512]{3,2,1,0:T(8,128)(2,1)} %turb_ref.1, f32[8]{0:T(128)} %wind_in.1, f32[16,512]{1,0:T(8,128)} %adm_in.1, s32[16,512]{1,0:T(8,128)} %kind_in.1, s32[2,8]{1,0:T(2,128)} %cells_in.1, s32[2,8]{1,0:T(2,128)} %eighths_in.1), custom_call_target="tpu_custom_call" | custom-call | tf_op jit(solution)/shard_map/pallas_call | solution.py:419
  41.0 2.3 %copy.9 = f32[4,8,16,512]{3,2,1,0:T(8,128)} copy(f32[4,8,16,512]{3,2,1,0:T(8,128)} %shard_map.73) | data formatting | bytes 2097152

commit v3 on v2

--- a/solution.py
+++ b/solution.py
@@ -20,7 +20,7 @@
     state_ref, turb_ref, wind_in, adm_in, kind_in, cells_in, eighths_in,
     out_ref,
     wind_ref, adm_ref, kind_ref, cells_ref, eighths_ref,
-    pa, ua, va, wa, pb, ub, vb, wb, chg, adv, sqr, gath, outb, froz,
+    pa, ua, va, wa, pb, ub, vb, wb, chg, adv, sqr, gath, share, outb, froz,
     rsend, rrecv, hsend, hrecv,
     in_sem, out_sem, s1, r1, s2, r2, rs, rr, hs, hr,
 ):
@@ -32,12 +32,16 @@
     half = levels // 2
 
     def part(j):
-        field = j // (levels * pieces)
-        rest = j % (levels * pieces)
-        return field, rest // pieces, pl.multiple_of((rest % pieces) * width, width)
+        field = jnp.where(j >= levels * pieces, 1, 0)
+        rest = j - field * (levels * pieces)
+        if pieces == 1:
+            return field, rest, 0
+        level = lax.div(rest, pieces)
+        return field, level, pl.multiple_of((rest - level * pieces) * width, width)
 
     def peer(k):
-        return lax.rem(me + k, n)
+        j = me + k
+        return jnp.where(j >= n, j - n, j)
 
     def rows_of(j):
         return pl.ds(pl.multiple_of(j * rows, rows), rows)
@@ -95,20 +99,31 @@
         return pltpu.make_async_remote_copy(
             src_ref=turb_ref.at[field, level, :, pl.ds(at, width)],
             dst_ref=gath.at[rows_of(me)],
-            send_sem=s1.at[to],
-            recv_sem=r1.at[me],
+            send_sem=s1,
+            recv_sem=r1,
             device_id={"cross": to},
             device_id_type=MESH,
         )
 
-    def gather_wait(k):
-        source = peer(k)
-        return pltpu.make_async_remote_copy(
-            src_ref=gath.at[rows_of(source)],
-            dst_ref=gath.at[rows_of(source)],
-            send_sem=s1.at[source],
-            recv_sem=r1.at[source],
-            device_id={"cross": source},
+    all_but_one = pl.ds(0, (n - 1) * rows)
+
+    def gather_all():
+        return pltpu.make_async_remote_copy(
+            src_ref=gath.at[all_but_one],
+            dst_ref=gath.at[all_but_one],
+            send_sem=s1,
+            recv_sem=r1,
+            device_id={"cross": peer(1)},
+            device_id_type=MESH,
+        )
+
+    def spread_all(step):
+        return pltpu.make_async_remote_copy(
+            src_ref=outb.at[step, all_but_one],
+            dst_ref=outb.at[step, all_but_one],
+            send_sem=s2.at[step],
+            recv_sem=r2.at[step],
+            device_id={"cross": peer(1)},
             device_id_type=MESH,
         )
 
@@ -219,59 +234,52 @@
     send_up(0, pa, wa)
     send_rows(0, 1)
 
-    own.wait()
-
-    def whole(k, carry):
-        gather_wait(k).wait_recv()
-        return carry
-
-    lax.fori_loop(1, n, whole, 0)
+
     block = math.gcd(length, 256)
-
-    def spread_copy(step, k):
-        to = peer(k)
-        return pltpu.make_async_remote_copy(
-            src_ref=outb.at[step, rows_of(to)],
-            dst_ref=froz.at[step, my_field, my_level, :, pl.ds(my_at, width)],
-            send_sem=s2.at[step, to],
-            recv_sem=r2.at[step, me],
-            device_id={"cross": to},
-            device_id_type=MESH,
-        )
-
-    def spread_wait(step, k):
-        source = peer(k)
-        field, level, at = part(source)
-        return pltpu.make_async_remote_copy(
-            src_ref=outb.at[step, rows_of(source)],
-            dst_ref=froz.at[step, field, level, :, pl.ds(at, width)],
-            send_sem=s2.at[step, source],
-            recv_sem=r2.at[step, source],
-            device_id={"cross": source},
-            device_id_type=MESH,
-        )
-
-    def spread_some(step, third, of):
-        def spread(k, carry):
-            spread_copy(step, k).start()
-            return carry
-
-        lax.fori_loop(1 + (n - 1) * third // of, 1 + (n - 1) * (third + 1) // of, spread, 0)
 
     for step in range(steps):
         cells = cells_ref[step, my_level]
         weight = eighths_ref[step, my_level].astype(jnp.float32) / 8.0
 
-        def mix(i, carry, step=step, cells=cells, weight=weight):
+        def weigh(i, carry, step=step, cells=cells, weight=weight):
             top = pl.multiple_of(i * block, block)
             to_row = lax.broadcasted_iota(jnp.int32, (block, length), 0) + top
             from_row = lax.broadcasted_iota(jnp.int32, (block, length), 1)
             back = to_row - from_row - cells
             back = jnp.where(back < 0, back + length, back)
             back = jnp.where(back < 0, back + length, back)
-            share = jnp.where(back == 0, 1.0 - weight, jnp.where(back == 1, weight, 0.0))
+            mix = jnp.where(back == 0, 1.0 - weight, jnp.where(back == 1, weight, 0.0))
+            share[step, pl.ds(top, block)] = mix.astype(jnp.bfloat16)
+            return carry
+
+        lax.fori_loop(0, length // block, weigh, 0)
+
+    own.wait()
+    gather_all().wait_recv()
+
+    def spread_copy(step, k):
+        to = peer(k)
+        return pltpu.make_async_remote_copy(
+            src_ref=outb.at[step, rows_of(to)],
+            dst_ref=froz.at[step, my_field, my_level, :, pl.ds(my_at, width)],
+            send_sem=s2.at[step],
+            recv_sem=r2.at[step],
+            device_id={"cross": to},
+            device_id_type=MESH,
+        )
+
+    def spread_some(step, third, of):
+        def spread(k, carry):
+            spread_copy(step, k).start()
+            return carry
+
+        lax.fori_loop(1 + (n - 1) * third // of, 1 + (n - 1) * (third + 1) // of, spread, 0)
+
+    for step in range(steps):
+        def mix(i, carry, step=step):
+            top = pl.multiple_of(i * block, block)
             outb[step, pl.ds(top, block)] = jnp.dot(
-                share.astype(jnp.bfloat16), gath[...], preferred_element_type=jnp.float32
+                share[step, pl.ds(top, block)], gath[...], preferred_element_type=jnp.float32
             ).astype(jnp.bfloat16)
             return carry
 
@@ -304,11 +312,7 @@
         pn, un, vn, wn = sets[(k + 1) % 2]
         last = k == sections - 1
         if section == 0:
-            def arrive(j, carry, step=step):
-                spread_wait(step, j).wait_recv()
-                return carry
-
-            lax.fori_loop(1, n, arrive, 0)
+            spread_all(step).wait_recv()
         if step + 1 < steps:
             spread_some(step + 1, section, 3)
         receive_below(k, po, wo)
@@ -387,13 +391,9 @@
 
     lax.fori_loop(0, levels, stored, 0)
 
-    def left(k, carry):
-        gather_copy(k).wait_send()
-        for step in range(steps):
-            spread_copy(step, k).wait_send()
-        return carry
-
-    lax.fori_loop(1, n, left, 0)
+    gather_all().wait_send()
+    for step in range(steps):
+        spread_all(step).wait_send()
     for k in range(sections):
         for side, there in ((0, has_left), (1, has_right)):
             @pl.when(there)
@@ -433,6 +433,7 @@
             plain,
             plain,
             pltpu.VMEM((n * rows, width), bf16),
+            pltpu.VMEM((steps, n * rows, n * rows), bf16),
             pltpu.VMEM((steps, n * rows, width), bf16),
             pltpu.VMEM((steps, 2, levels, rows, cols), bf16),
             pltpu.VMEM((sections, 2, 2 * levels, cols), f32),
@@ -440,8 +441,8 @@
             pltpu.VMEM((sections, 2, 2, rows, cols), bf16),
             pltpu.VMEM((sections, 2, 2, rows, cols), bf16),
             dma((10,)), dma((levels,)),
-            dma((n,)), dma((n,)),
-            dma((steps, n)), dma((steps, n)),
+            dma, dma,
+            dma((steps,)), dma((steps,)),
             dma((sections, 2, 2)), dma((sections, 2, 2)),
             dma((sections, 2)), dma((sections, 2)),
         ],

time: 43.8 us -> 42.8 us (0.977)
  Pallas kernels: 40.9 us -> 39.9 us
    pallas_call x1, Pallas kernels: 40.9 us -> 39.9 us  [body(): pl.pallas_call(functools.partial(kernel, n, floors, steps, levels, rows,...]
where the time goes in v3:
time: 42.8 us; the launch traced here: 42.2 us
  Pallas kernels  39.9 us (93%)
  local copies, waits for them, and re-layouts  2.31 us (5%)
    pallas_call x1, Pallas kernels, body(): pl.pallas_call(functools.partial(kernel, n, floors, steps, levels, rows,...  39.9 us
    unnamed x1, local copies, waits for them, and re-layouts  2.31 us

profile of v3, /device:TPU:13, one launch (start us, length us, event | category | flops | bytes accessed | tf_op | source)
XLA Modules:
  0.0 42.2 jit_solution(14211413042459527368)
XLA Ops:
  0.0 39.9 %shard_map.73 = f32[4,8,16,512]{3,2,1,0:T(8,128)} custom-call(f32[4,8,16,512]{3,2,1,0:T(8,128)} %state_ref.1, bf16[2,8,16,512]{3,2,1,0:T(8,128)(2,1)} %turb_ref.1, f32[8]{0:T(128)} %wind_in.1, f32[16,512]{1,0:T(8,128)} %adm_in.1, s32[16,512]{1,0:T(8,128)} %kind_in.1, s32[2,8]{1,0:T(2,128)} %cells_in.1, s32[2,8]{1,0:T(2,128)} %eighths_in.1), custom_call_target="tpu_custom_call" | custom-call | tf_op jit(solution)/shard_map/pallas_call | solution.py:419
  39.9 2.3 %copy.9 = f32[4,8,16,512]{3,2,1,0:T(8,128)} copy(f32[4,8,16,512]{3,2,1,0:T(8,128)} %shard_map.73) | data formatting | bytes 2097152

commit v4 on v3

--- a/solution.py
+++ b/solution.py
@@ -381,7 +381,7 @@
 
             return carry
 
-        lax.fori_loop(0, levels, update, 0)
+        lax.fori_loop(0, levels, update, 0, unroll=2)
         if not last:
             send_rows(k + 1, 1)
 

time: 42.8 us -> 42.7 us (level)
  no operation moved by 1% of the time
where the time goes in v4:
time: 42.7 us; the launch traced here: 42.2 us
  Pallas kernels  39.8 us (93%)
  local copies, waits for them, and re-layouts  2.31 us (5%)
    pallas_call x1, Pallas kernels, body(): pl.pallas_call(functools.partial(kernel, n, floors, steps, levels, rows,...  39.8 us
    unnamed x1, local copies, waits for them, and re-layouts  2.31 us

profile of v4, /device:TPU:13, one launch (start us, length us, event | category | flops | bytes accessed | tf_op | source)
XLA Modules:
  0.0 42.2 jit_solution(13350484462092807729)
XLA Ops:
  0.0 39.8 %shard_map.73 = f32[4,8,16,512]{3,2,1,0:T(8,128)} custom-call(f32[4,8,16,512]{3,2,1,0:T(8,128)} %state_ref.1, bf16[2,8,16,512]{3,2,1,0:T(8,128)(2,1)} %turb_ref.1, f32[8]{0:T(128)} %wind_in.1, f32[16,512]{1,0:T(8,128)} %adm_in.1, s32[16,512]{1,0:T(8,128)} %kind_in.1, s32[2,8]{1,0:T(2,128)} %cells_in.1, s32[2,8]{1,0:T(2,128)} %eighths_in.1), custom_call_target="tpu_custom_call" | custom-call | tf_op jit(solution)/shard_map/pallas_call | solution.py:419
  39.8 2.3 %copy.9 = f32[4,8,16,512]{3,2,1,0:T(8,128)} copy(f32[4,8,16,512]{3,2,1,0:T(8,128)} %shard_map.73) | data formatting | bytes 2097152
